TPU v7x, 512 devices: a whole 4x8x8 slice. The times are simulated.
512 devices in a mesh: gx: 8 (over z), gy: 8 (over x, core), gz: 8 (over y).
Axes of the slice: x: 4, y: 8, z: 8, core: 2. Of those that a mesh axis runs over, the one named last changes fastest.
Arguments:
- basis: bfloat16 [3584, 64, 4096], P(('gx', 'gy', 'gz')), may hold values from -6 to 6
- density_blocks: bfloat16 [24576, 4096], P(('gx', 'gy', 'gz')), may hold values from -0.014953613 to 0.014953613
- pair_groups: int32 [2, 24576], P(None, ('gx', 'gy', 'gz')), may hold values from 0 to 6, as said below
- owner: int32 [24576, 1], P(('gx', 'gy', 'gz')), may hold values from 0 to 63; in each aligned block of 48 rows (0 to 47, 48 to 95, ...) at most 2 rows name the same one
- owner_slot: int32 [24576], P(('gx', 'gy', 'gz')), may hold values from 0 to 47
Outputs:
- ks_blocks: bfloat16 [24576, 4096], P(('gx', 'gy', 'gz'))
- xc_potential: float32 [64, 64, 64], P('gx', 'gy', 'gz')
Inputs may be any that keep to these rules, and one draw needn't show every extreme that they name: At most 2 pairs of one subdomain name the same owner, and in every draw some subdomain's pairs name one owner exactly 2 times; every owner is named by some pair. `pair_groups`: the pairs of one subdomain are distinct ordered pairs of its groups.
All inputs are finite; a program needn't handle non-finite values.
Results may differ from a plain program's by a relative error of at most 0.0055.
Values may be sent and summed in bfloat16 or wider, within the bound.
A program may use at most 64 MiB of HBM per device.

v0:
```python
import jax
import jax.numpy as jnp
from jax import lax
from jax.sharding import PartitionSpec as P

BASIS = 64
CELLS = 8
RIM = 4
EXT = 16
EXT3 = 4096


XC_COEF = 0.9847450218426965
GRID_WEIGHT = 0.015625


def extended(cells, sides, width):
    for axis, dim in sides:
        count = lax.axis_size(axis)
        head = lax.slice_in_dim(cells, 0, width, axis=dim)
        tail = lax.slice_in_dim(cells, cells.shape[dim] - width, cells.shape[dim], axis=dim)
        cells = jnp.concatenate(
            [
                lax.ppermute(tail, axis, [(i, (i + 1) % count) for i in range(count)]),
                cells,
                lax.ppermute(head, axis, [((i + 1) % count, i) for i in range(count)]),
            ],
            axis=dim,
        )
    return cells


def slater_potential(density):
    return -XC_COEF * density / jnp.cbrt(density * density + 1.0)


def fold_axis(padded, dimension):
    lower = lax.slice_in_dim(padded, 0, RIM, axis=dimension)
    middle = lax.slice_in_dim(padded, 2 * RIM, 2 * RIM + CELLS, axis=dimension)
    upper = lax.slice_in_dim(padded, CELLS + 3 * RIM, CELLS + 4 * RIM, axis=dimension)
    widths_low = [
        (0, CELLS - RIM) if position == dimension else (0, 0) for position in range(padded.ndim)
    ]
    widths_high = [
        (CELLS - RIM, 0) if position == dimension else (0, 0) for position in range(padded.ndim)
    ]
    return middle + jnp.pad(lower, widths_low) + jnp.pad(upper, widths_high)


def per_device(basis, density_blocks, pair_groups, owner, owner_slot):
    groups = basis.shape[0]
    pairs = density_blocks.shape[0]
    square = BASIS * BASIS
    pair_codes = pair_groups[0] * groups + pair_groups[1]
    code_match = (
        pair_codes[:, None] == jnp.arange(groups * groups, dtype=jnp.int32)[None, :]
    ).astype(jnp.bfloat16)
    dense_blocks = lax.dot_general(
        code_match, density_blocks, (((0,), (0,)), ((), ())), preferred_element_type=jnp.float32
    ).astype(jnp.bfloat16)
    matrix = (
        dense_blocks.reshape(groups, groups, BASIS, BASIS)
        .transpose(0, 2, 1, 3)
        .reshape(groups * BASIS, groups * BASIS)
    )
    stacked = basis.reshape(groups * BASIS, EXT3)
    projected = jnp.dot(matrix, stacked, preferred_element_type=jnp.float32)
    box_density = jnp.sum(stacked.astype(jnp.float32) * projected, axis=0).reshape(EXT, EXT, EXT)
    along_x = fold_axis(extended(box_density, (("gx", 0),), RIM), 0)
    along_y = fold_axis(extended(along_x, (("gy", 1),), RIM), 1)
    density = fold_axis(extended(along_y, (("gz", 2),), RIM), 2)
    potential = slater_potential(density)
    potential_ext = extended(potential, (("gx", 0), ("gy", 1), ("gz", 2)), RIM).reshape(EXT3)
    weighted = (stacked.astype(jnp.float32) * potential_ext[None, :]).astype(jnp.bfloat16)
    ks_full = (
        lax.dot_general(
            weighted, stacked, (((1,), (1,)), ((), ())), preferred_element_type=jnp.float32
        )
        * GRID_WEIGHT
    )
    ks_table = (
        ks_full.reshape(groups, BASIS, groups, BASIS)
        .transpose(0, 2, 1, 3)
        .reshape(groups * groups, square)
    )
    pair_blocks = jnp.take(ks_table, pair_codes, axis=0).astype(jnp.bfloat16)
    rows_x = lax.axis_size("gx")
    rows_y = lax.axis_size("gy")
    owners = rows_x * rows_y
    capacity = max(2, 2 * pairs // owners)
    owner_ids = owner[:, 0]
    order_ids = jnp.arange(pairs, dtype=jnp.int32)
    earlier = (owner_ids[:, None] == owner_ids[None, :]) & (order_ids[:, None] > order_ids[None, :])
    rank_within = jnp.sum(earlier.astype(jnp.int32), axis=1)
    positions = owner_ids * capacity + rank_within
    slot_match = jnp.arange(owners * capacity, dtype=jnp.int32)[:, None] == positions[None, :]
    send_blocks = jnp.dot(
        slot_match.astype(jnp.bfloat16), pair_blocks, preferred_element_type=jnp.float32
    ).astype(jnp.bfloat16)
    send_slots = jnp.sum(jnp.where(slot_match, owner_slot[None, :] + 1, 0), axis=1) - 1
    got_blocks, got_slots = (
        lax.all_to_all(
            send_blocks.reshape(owners, capacity, square),
            ("gx", "gy"),
            split_axis=0,
            concat_axis=0,
            tiled=True,
        ),
        lax.all_to_all(
            send_slots.reshape(owners, capacity),
            ("gx", "gy"),
            split_axis=0,
            concat_axis=0,
            tiled=True,
        ),
    )
    got_blocks = got_blocks.reshape(owners * capacity, square)
    got_slots = got_slots.reshape(owners * capacity)
    store_match = (jnp.arange(pairs, dtype=jnp.int32)[:, None] == got_slots[None, :]).astype(
        jnp.bfloat16
    )
    ks_blocks = jnp.dot(store_match, got_blocks, preferred_element_type=jnp.float32).astype(
        jnp.bfloat16
    )
    return (ks_blocks, potential)


def solution(mesh):
    return jax.shard_map(
        per_device,
        mesh=mesh,
        in_specs=(
            P(("gx", "gy", "gz"), None, None),
            P(("gx", "gy", "gz"), None),
            P(None, ("gx", "gy", "gz")),
            P(("gx", "gy", "gz"), None),
            P(("gx", "gy", "gz")),
        ),
        out_specs=(P(("gx", "gy", "gz"), None), P("gx", "gy", "gz")),
        check_vma=False,
    )
```

profile of v0, /device:TPU:16, one launch (start us, length us, event | category | flops | bytes accessed | tf_op | source)
XLA Modules:
  0.0 121.4 jit_solution(18343151688907381833)
XLA Ops:
  0.6 0.8 compare_and_fusion
  2.1 0.9 reshape.139
  2.9 0.6 copy.17
  4.0 5.2 %multiply_reduce_fusion = f32[4096]{0:T(1024)S(1)} fusion(bf16[448,4096]{1,0:T(8,128)(2,1)} %bitcast.23, bf16[448,448]{1,0:T(8,128)(2,1)S(1)} %reshape.140), kind=kOutput, calls=%fused_computation.2 | convolution fusion | flops 1649668096 | bytes 4087808 | tf_op jit(solution)/shard_map/dot_general | solution.py:67
  9.3 4.3 %collective-permute-start = (f32[4,16,16]{2,1,0:T(8,128)S(1)}, f32[4,16,16]{2,1,0:T(8,128)S(1)}, u32[]{:S(2)}, u32[]{:S(2)}) collective-permute-start(f32[4,16,16]{2,1,0:T(8,128)S(1)} %slice.89), channel_id=1, source_target_pairs={{0,64},{64,128},{128,192},{192,256},{256,320},{320,384},{384,448},... | collective-permute-start | bytes 12296 | tf_op jit(solution)/shard_map/ppermute | solution.py:24
  13.6 8.6 %collective-permute-start.1 = (f32[4,16,16]{2,1,0:T(8,128)S(1)}, f32[4,16,16]{2,1,0:T(8,128)S(1)}, u32[]{:S(2)}, u32[]{:S(2)}) collective-permute-start(f32[4,16,16]{2,1,0:T(8,128)S(1)} %slice.91), channel_id=1, source_target_pairs={{64,0},{128,64},{192,128},{256,192},{320,256},{384,320},{448,384},... | collective-permute-start | bytes 12296 | tf_op jit(solution)/shard_map/ppermute | solution.py:26
  22.5 1.3 %collective-permute-done.1 = f32[4,16,16]{2,1,0:T(8,128)S(1)} collective-permute-done((f32[4,16,16]{2,1,0:T(8,128)S(1)}, f32[4,16,16]{2,1,0:T(8,128)S(1)}, u32[]{:S(2)}, u32[]{:S(2)}) %collective-permute-start.1) | collective-permute-done | bytes 4128 | tf_op jit(solution)/shard_map/ppermute | solution.py:26
  23.9 2.9 %collective-permute-start.3 = (f32[8,4,16]{2,1,0:T(4,128)S(1)}, f32[8,4,16]{2,1,0:T(4,128)S(1)}, u32[]{:S(2)}, u32[]{:S(2)}) collective-permute-start(f32[8,4,16]{2,1,0:T(4,128)S(1)} %get-tuple-element.9), channel_id=1, source_target_pairs={{8,0},{16,8},{24,16},{32,24},{40,32},{48,40},{56,48},{0,56},{9,1},... | collective-permute-start | bytes 6152 | tf_op jit(solution)/shard_map/ppermute | solution.py:26
  26.8 1.4 %collective-permute-done.2 = f32[8,4,16]{2,1,0:T(4,128)S(1)} collective-permute-done((f32[8,4,16]{2,1,0:T(4,128)S(1)}, f32[8,4,16]{2,1,0:T(4,128)S(1)}, u32[]{:S(2)}, u32[]{:S(2)}) %collective-permute-start.2) | collective-permute-done | bytes 2080 | tf_op jit(solution)/shard_map/ppermute | solution.py:24
  28.3 3.5 %collective-permute-start.4 = (f32[8,8,4]{2,1,0:T(8,128)S(1)}, f32[8,8,4]{2,1,0:T(8,128)S(1)}, u32[]{:S(2)}, u32[]{:S(2)}) collective-permute-start(f32[8,8,4]{2,1,0:T(8,128)S(1)} %get-tuple-element.12), channel_id=1, source_target_pairs={{0,1},{1,2},{2,3},{3,4},{4,5},{5,6},{6,7},{7,0},{8,9},{9,10},{10,1... | collective-permute-start | bytes 3080 | tf_op jit(solution)/shard_map/ppermute | solution.py:24
  31.9 2.4 %collective-permute-start.5 = (f32[8,8,4]{2,1,0:T(8,128)S(1)}, f32[8,8,4]{2,1,0:T(8,128)S(1)}, u32[]{:S(2)}, u32[]{:S(2)}) collective-permute-start(f32[8,8,4]{2,1,0:T(8,128)S(1)} %get-tuple-element.13), channel_id=1, source_target_pairs={{1,0},{2,1},{3,2},{4,3},{5,4},{6,5},{7,6},{0,7},{9,8},{10,9},{11,1... | collective-permute-start | bytes 3080 | tf_op jit(solution)/shard_map/ppermute | solution.py:26
  34.3 4.1 %collective-permute-done.5 = f32[8,8,4]{2,1,0:T(8,128)S(1)} collective-permute-done((f32[8,8,4]{2,1,0:T(8,128)S(1)}, f32[8,8,4]{2,1,0:T(8,128)S(1)}, u32[]{:S(2)}, u32[]{:S(2)}) %collective-permute-start.5) | collective-permute-done | bytes 1056 | tf_op jit(solution)/shard_map/ppermute | solution.py:26
  38.6 1.9 %collective-permute-start.6 = (f32[4,8,8]{2,1,0:T(8,128)S(1)}, f32[4,8,8]{2,1,0:T(8,128)S(1)}, u32[]{:S(2)}, u32[]{:S(2)}) collective-permute-start(f32[4,8,8]{2,1,0:T(8,128)S(1)} %get-tuple-element.10), channel_id=1, source_target_pairs={{0,64},{64,128},{128,192},{192,256},{256,320},{320,384},{384,448},... | collective-permute-start | bytes 3080 | tf_op jit(solution)/shard_map/ppermute | solution.py:24
  40.5 5.4 %collective-permute-start.7 = (f32[4,8,8]{2,1,0:T(8,128)S(1)}, f32[4,8,8]{2,1,0:T(8,128)S(1)}, u32[]{:S(2)}, u32[]{:S(2)}) collective-permute-start(f32[4,8,8]{2,1,0:T(8,128)S(1)} %get-tuple-element.11), channel_id=1, source_target_pairs={{64,0},{128,64},{192,128},{256,192},{320,256},{384,320},{448,384},... | collective-permute-start | bytes 3080 | tf_op jit(solution)/shard_map/ppermute | solution.py:26
  46.0 0.8 sub.7
  46.7 7.0 %all-to-all-start = ((s32[64,1,2]{2,1,0:T(1,128)}), s32[64,1,2]{2,1,0:T(1,128)S(1)}, u32[]{:S(2)}, u32[]{:S(2)}) async-start(s32[64,1,2]{2,1,0:T(1,128)} %bitcast.1), calls=%async_computation | async-start | bytes 65536 | tf_op jit(solution)/shard_map/all_to_all | solution.py:109
  53.9 2.9 %collective-permute-start.9 = (f32[16,4,8]{2,1,0:T(4,128)S(1)}, f32[16,4,8]{2,1,0:T(4,128)S(1)}, u32[]{:S(2)}, u32[]{:S(2)}) collective-permute-start(f32[16,4,8]{2,1,0:T(4,128)S(1)} %get-tuple-element.7), channel_id=1, source_target_pairs={{8,0},{16,8},{24,16},{32,24},{40,32},{48,40},{56,48},{0,56},{9,1},... | collective-permute-start | bytes 6152 | tf_op jit(solution)/shard_map/ppermute | solution.py:26
  56.8 1.6 %collective-permute-done.8 = f32[16,4,8]{2,1,0:T(4,128)S(1)} collective-permute-done((f32[16,4,8]{2,1,0:T(4,128)S(1)}, f32[16,4,8]{2,1,0:T(4,128)S(1)}, u32[]{:S(2)}, u32[]{:S(2)}) %collective-permute-start.8) | collective-permute-done | bytes 2080 | tf_op jit(solution)/shard_map/ppermute | solution.py:24
  58.5 5.4 %collective-permute-start.10 = (f32[16,16,4]{2,1,0:T(8,128)S(1)}, f32[16,16,4]{2,1,0:T(8,128)S(1)}, u32[]{:S(2)}, u32[]{:S(2)}) collective-permute-start(f32[16,16,4]{2,1,0:T(8,128)S(1)} %get-tuple-element.4), channel_id=1, source_target_pairs={{0,1},{1,2},{2,3},{3,4},{4,5},{5,6},{6,7},{7,0},{8,9},{9,10},{10,1... | collective-permute-start | bytes 12296 | tf_op jit(solution)/shard_map/ppermute | solution.py:24
  63.9 1.9 %collective-permute-start.11 = (f32[16,16,4]{2,1,0:T(8,128)S(1)}, f32[16,16,4]{2,1,0:T(8,128)S(1)}, u32[]{:S(2)}, u32[]{:S(2)}) collective-permute-start(f32[16,16,4]{2,1,0:T(8,128)S(1)} %get-tuple-element.5), channel_id=1, source_target_pairs={{1,0},{2,1},{3,2},{4,3},{5,4},{6,5},{7,6},{0,7},{9,8},{10,9},{11,1... | collective-permute-start | bytes 12296 | tf_op jit(solution)/shard_map/ppermute | solution.py:26
  65.9 1.7 %collective-permute-done.10 = f32[16,16,4]{2,1,0:T(8,128)S(1)} collective-permute-done((f32[16,16,4]{2,1,0:T(8,128)S(1)}, f32[16,16,4]{2,1,0:T(8,128)S(1)}, u32[]{:S(2)}, u32[]{:S(2)}) %collective-permute-start.10) | collective-permute-done | bytes 4128 | tf_op jit(solution)/shard_map/ppermute | solution.py:24
  67.6 4.1 %collective-permute-done.11 = f32[16,16,4]{2,1,0:T(8,128)S(1)} collective-permute-done((f32[16,16,4]{2,1,0:T(8,128)S(1)}, f32[16,16,4]{2,1,0:T(8,128)S(1)}, u32[]{:S(2)}, u32[]{:S(2)}) %collective-permute-start.11) | collective-permute-done | bytes 4128 | tf_op jit(solution)/shard_map/ppermute | solution.py:26
  72.0 3.1 %multiply_convert_fusion = bf16[7,64,4096]{2,1,0:T(8,128)(2,1)S(1)} fusion(bf16[7,64,4096]{2,1,0:T(8,128)(2,1)} %param.5, f32[4096]{0:T(1024)S(1)} %mul.67), kind=kLoop, calls=%fused_computation.1 | loop fusion | flops 5505024 | bytes 7356416 | tf_op jit(solution)/shard_map/convert_element_type | solution.py:74
  75.1 2.1 %convolution_multiply_fusion = bf16[448,448]{1,0:T(8,128)(2,1)S(1)} fusion(bf16[448,4096]{1,0:T(8,128)(2,1)S(1)} %bitcast.25, bf16[448,4096]{1,0:T(8,128)(2,1)S(1)} %bitcast.24), kind=kOutput, calls=%fused_computation.6 | convolution fusion | flops 1644568576 | bytes 7741440 | tf_op jit(solution)/shard_map/dot_general | solution.py:76
  77.2 0.5 reshape.141
  78.0 0.7 reshape.142
  78.7 0.8 gather_fusion
  80.0 1.5 %reshape.143 = bf16[64,2,4096]{2,1,0:T(2,128)(2,1)} reshape(bf16[128,4096]{1,0:T(8,128)(2,1)S(1)} %convolution_convert_fusion) | data formatting | bytes 2097152 | tf_op jit(solution)/shard_map/reshape | solution.py:103
  81.5 9.5 %all-to-all-start.1 = ((bf16[64,2,4096]{2,1,0:T(2,128)(2,1)}), bf16[64,2,4096]{2,1,0:T(2,128)(2,1)S(1)}, u32[]{:S(2)}, u32[]{:S(2)}) async-start(bf16[64,2,4096]{2,1,0:T(2,128)(2,1)} %reshape.143), calls=%async_computation.1 | async-start | bytes 2097152 | tf_op jit(solution)/shard_map/all_to_all | solution.py:102
  91.5 0.7 reduce.3
  92.4 27.5 %all-to-all-done.1 = bf16[64,2,4096]{2,1,0:T(2,128)(2,1)S(1)} async-done(((bf16[64,2,4096]{2,1,0:T(2,128)(2,1)}), bf16[64,2,4096]{2,1,0:T(2,128)(2,1)S(1)}, u32[]{:S(2)}, u32[]{:S(2)}) %all-to-all-start.1) | async-done | bytes 1048608 | tf_op jit(solution)/shard_map/all_to_all | solution.py:102
  120.3 1.0 convolution_convert_fusion.2
  (49 shorter events, 4.2 us)
Async XLA Ops:
  0.6 1.0 copy-start
  3.9 18.3 %copy-start.3 = (s32[48,1]{0,1:T(1,128)S(1)}, s32[48,1]{0,1:T(1,128)}, u32[]{:S(2)}) copy-start(s32[48,1]{0,1:T(1,128)} %param.8) | copy-start | bytes 580
  3.9 22.9 %copy-start.4 = (s32[48]{0:T(128)S(1)}, s32[48]{0:T(128)}, u32[]{:S(2)}) copy-start(s32[48]{0:T(128)} %param.9) | copy-start | bytes 580
  9.3 13.2 %collective-permute-start = (f32[4,16,16]{2,1,0:T(8,128)S(1)}, f32[4,16,16]{2,1,0:T(8,128)S(1)}, u32[]{:S(2)}, u32[]{:S(2)}) collective-permute-start(f32[4,16,16]{2,1,0:T(8,128)S(1)} %slice.89), channel_id=1, source_target_pairs={{0,64},{64,128},{128,192},{192,256},{256,320},{320,384},{384,448},... | collective-permute-start | bytes 12296 | tf_op jit(solution)/shard_map/ppermute | solution.py:24
  13.6 10.2 %collective-permute-start.1 = (f32[4,16,16]{2,1,0:T(8,128)S(1)}, f32[4,16,16]{2,1,0:T(8,128)S(1)}, u32[]{:S(2)}, u32[]{:S(2)}) collective-permute-start(f32[4,16,16]{2,1,0:T(8,128)S(1)} %slice.91), channel_id=1, source_target_pairs={{64,0},{128,64},{192,128},{256,192},{320,256},{384,320},{448,384},... | collective-permute-start | bytes 12296 | tf_op jit(solution)/shard_map/ppermute | solution.py:26
  23.8 4.4 %collective-permute-start.2 = (f32[8,4,16]{2,1,0:T(4,128)S(1)}, f32[8,4,16]{2,1,0:T(4,128)S(1)}, u32[]{:S(2)}, u32[]{:S(2)}) collective-permute-start(f32[8,4,16]{2,1,0:T(4,128)S(1)} %get-tuple-element.8), channel_id=1, source_target_pairs={{0,8},{8,16},{16,24},{24,32},{32,40},{40,48},{48,56},{56,0},{1,9},... | collective-permute-start | bytes 6152 | tf_op jit(solution)/shard_map/ppermute | solution.py:24
  23.9 4.4 %collective-permute-start.3 = (f32[8,4,16]{2,1,0:T(4,128)S(1)}, f32[8,4,16]{2,1,0:T(4,128)S(1)}, u32[]{:S(2)}, u32[]{:S(2)}) collective-permute-start(f32[8,4,16]{2,1,0:T(4,128)S(1)} %get-tuple-element.9), channel_id=1, source_target_pairs={{8,0},{16,8},{24,16},{32,24},{40,32},{48,40},{56,48},{0,56},{9,1},... | collective-permute-start | bytes 6152 | tf_op jit(solution)/shard_map/ppermute | solution.py:26
  28.3 6.0 %collective-permute-start.4 = (f32[8,8,4]{2,1,0:T(8,128)S(1)}, f32[8,8,4]{2,1,0:T(8,128)S(1)}, u32[]{:S(2)}, u32[]{:S(2)}) collective-permute-start(f32[8,8,4]{2,1,0:T(8,128)S(1)} %get-tuple-element.12), channel_id=1, source_target_pairs={{0,1},{1,2},{2,3},{3,4},{4,5},{5,6},{6,7},{7,0},{8,9},{9,10},{10,1... | collective-permute-start | bytes 3080 | tf_op jit(solution)/shard_map/ppermute | solution.py:24
  31.9 6.6 %collective-permute-start.5 = (f32[8,8,4]{2,1,0:T(8,128)S(1)}, f32[8,8,4]{2,1,0:T(8,128)S(1)}, u32[]{:S(2)}, u32[]{:S(2)}) collective-permute-start(f32[8,8,4]{2,1,0:T(8,128)S(1)} %get-tuple-element.13), channel_id=1, source_target_pairs={{1,0},{2,1},{3,2},{4,3},{5,4},{6,5},{7,6},{0,7},{9,8},{10,9},{11,1... | collective-permute-start | bytes 3080 | tf_op jit(solution)/shard_map/ppermute | solution.py:26
  38.6 36.5 %copy-start.2 = (f32[8,8,8]{2,1,0:T(8,128)}, f32[8,8,8]{2,1,0:T(8,128)S(1)}, u32[]{:S(2)}) copy-start(f32[8,8,8]{2,1,0:T(8,128)S(1)} %cbrt_divide_fusion) | copy-start | bytes 6148
  38.6 15.2 %collective-permute-start.6 = (f32[4,8,8]{2,1,0:T(8,128)S(1)}, f32[4,8,8]{2,1,0:T(8,128)S(1)}, u32[]{:S(2)}, u32[]{:S(2)}) collective-permute-start(f32[4,8,8]{2,1,0:T(8,128)S(1)} %get-tuple-element.10), channel_id=1, source_target_pairs={{0,64},{64,128},{128,192},{192,256},{256,320},{320,384},{384,448},... | collective-permute-start | bytes 3080 | tf_op jit(solution)/shard_map/ppermute | solution.py:24
  40.5 13.2 %collective-permute-start.7 = (f32[4,8,8]{2,1,0:T(8,128)S(1)}, f32[4,8,8]{2,1,0:T(8,128)S(1)}, u32[]{:S(2)}, u32[]{:S(2)}) collective-permute-start(f32[4,8,8]{2,1,0:T(8,128)S(1)} %get-tuple-element.11), channel_id=1, source_target_pairs={{64,0},{128,64},{192,128},{256,192},{320,256},{384,320},{448,384},... | collective-permute-start | bytes 3080 | tf_op jit(solution)/shard_map/ppermute | solution.py:26
  46.7 34.8 %all-to-all-start = ((s32[64,1,2]{2,1,0:T(1,128)}), s32[64,1,2]{2,1,0:T(1,128)S(1)}, u32[]{:S(2)}, u32[]{:S(2)}) async-start(s32[64,1,2]{2,1,0:T(1,128)} %bitcast.1), calls=%async_computation | async-start | bytes 65536 | tf_op jit(solution)/shard_map/all_to_all | solution.py:109
  53.8 4.6 %collective-permute-start.8 = (f32[16,4,8]{2,1,0:T(4,128)S(1)}, f32[16,4,8]{2,1,0:T(4,128)S(1)}, u32[]{:S(2)}, u32[]{:S(2)}) collective-permute-start(f32[16,4,8]{2,1,0:T(4,128)S(1)} %get-tuple-element.6), channel_id=1, source_target_pairs={{0,8},{8,16},{16,24},{24,32},{32,40},{40,48},{48,56},{56,0},{1,9},... | collective-permute-start | bytes 6152 | tf_op jit(solution)/shard_map/ppermute | solution.py:24
  53.9 4.5 %collective-permute-start.9 = (f32[16,4,8]{2,1,0:T(4,128)S(1)}, f32[16,4,8]{2,1,0:T(4,128)S(1)}, u32[]{:S(2)}, u32[]{:S(2)}) collective-permute-start(f32[16,4,8]{2,1,0:T(4,128)S(1)} %get-tuple-element.7), channel_id=1, source_target_pairs={{8,0},{16,8},{24,16},{32,24},{40,32},{48,40},{56,48},{0,56},{9,1},... | collective-permute-start | bytes 6152 | tf_op jit(solution)/shard_map/ppermute | solution.py:26
  58.5 9.1 %collective-permute-start.10 = (f32[16,16,4]{2,1,0:T(8,128)S(1)}, f32[16,16,4]{2,1,0:T(8,128)S(1)}, u32[]{:S(2)}, u32[]{:S(2)}) collective-permute-start(f32[16,16,4]{2,1,0:T(8,128)S(1)} %get-tuple-element.4), channel_id=1, source_target_pairs={{0,1},{1,2},{2,3},{3,4},{4,5},{5,6},{6,7},{7,0},{8,9},{9,10},{10,1... | collective-permute-start | bytes 12296 | tf_op jit(solution)/shard_map/ppermute | solution.py:24
  63.9 7.8 %collective-permute-start.11 = (f32[16,16,4]{2,1,0:T(8,128)S(1)}, f32[16,16,4]{2,1,0:T(8,128)S(1)}, u32[]{:S(2)}, u32[]{:S(2)}) collective-permute-start(f32[16,16,4]{2,1,0:T(8,128)S(1)} %get-tuple-element.5), channel_id=1, source_target_pairs={{1,0},{2,1},{3,2},{4,3},{5,4},{6,5},{7,6},{0,7},{9,8},{10,9},{11,1... | collective-permute-start | bytes 12296 | tf_op jit(solution)/shard_map/ppermute | solution.py:26
  72.0 3.1 %copy-start.1 = (bf16[7,64,4096]{2,1,0:T(8,128)(2,1)S(1)}, bf16[7,64,4096]{2,1,0:T(8,128)(2,1)}, u32[]{:S(2)}) copy-start(bf16[7,64,4096]{2,1,0:T(8,128)(2,1)} %param.5) | copy-start | bytes 11010052
  81.5 38.4 %all-to-all-start.1 = ((bf16[64,2,4096]{2,1,0:T(2,128)(2,1)}), bf16[64,2,4096]{2,1,0:T(2,128)(2,1)S(1)}, u32[]{:S(2)}, u32[]{:S(2)}) async-start(bf16[64,2,4096]{2,1,0:T(2,128)(2,1)} %reshape.143), calls=%async_computation.1 | async-start | bytes 2097152 | tf_op jit(solution)/shard_map/all_to_all | solution.py:102
where the time goes:
time: 122 us; the launch traced here: 121 us
  starting transfers between devices  55.8 us (46%)
  waiting for transfers between devices  41.8 us (34%)
  matrix products  9.29 us (8%)
  local copies, waits for them, and re-layouts  8.23 us (7%)
  other arithmetic  5.21 us (4%)
    all_to_all x1, waiting for transfers between devices, per_device(): lax.all_to_all(send_blocks.reshape(owners, capacity, square), ('gx', 'gy'...  27.5 us
    ppermute x6, starting transfers between devices, extended(): lax.ppermute(head, axis, [((i + 1) % count, i) for i in range(count)])  24.1 us
    ppermute x6, starting transfers between devices, extended(): lax.ppermute(tail, axis, [(i, (i + 1) % count) for i in range(count)])  15.2 us
    ppermute x6, waiting for transfers between devices, extended(): lax.ppermute(head, axis, [((i + 1) % count, i) for i in range(count)])  9.55 us
    all_to_all x1, starting transfers between devices, per_device(): lax.all_to_all(send_blocks.reshape(owners, capacity, square), ('gx', 'gy'...  9.49 us
    all_to_all x1, starting transfers between devices, per_device(): lax.all_to_all(send_slots.reshape(owners, capacity), ('gx', 'gy'), split_...  7 us
    dot_general x1, matrix products, per_device(): projected = jnp.dot(matrix, stacked, preferred_element_type=jnp.float32)  5.25 us
    ppermute x6, waiting for transfers between devices, extended(): lax.ppermute(tail, axis, [(i, (i + 1) % count) for i in range(count)])  4.76 us
  transfers between devices with their start and end apart: 14, of which 7 were waited for; matrix products, arithmetic and copies ran while one was open for 10% of the time, Pallas kernels for 0%

commit v1 on v0

v1 whole, which is shorter than its diff:
```python
import functools

import jax
import jax.numpy as jnp
from jax import lax
from jax.experimental import pallas as pl
from jax.experimental.pallas import tpu as pltpu
from jax.sharding import PartitionSpec as P

BASIS = 64
RIM = 4
EXT = 16
EXT3 = 4096
XC_COEF = 0.9847450218426965
GRID_WEIGHT = 0.015625
G = 7
ROWS = G * BASIS
WIDE = 512
N = 8
OWNERS = N * N
PAIRS = 48
CODES = 56
ROW_BLK = 32
MESH = pl.DeviceIdType.MESH
F32 = jnp.float32
BF16 = jnp.bfloat16

CHUNK = 512
NCHUNK = EXT3 // CHUNK

DIRS = [(a, b, c) for c in (0, 1, -1) for a in (0, 1, -1) for b in (0, 1, -1) if (a, b, c) != (0, 0, 0)]
DIR_ID = {d: n for n, d in enumerate(DIRS)}
OUT_PLANE = [d for d in DIRS if d[2] != 0]
PEERS = OWNERS - 1 + len(OUT_PLANE)
FAR_FIRST = (4, 3, 5, 2, 6, 1, 7, 0)


def half(step, low, high, whole):
    return whole if step == 0 else (high if step > 0 else low)


def bytes_wait(ref, sem):
    pltpu.make_async_copy(ref, ref, sem).wait()


def main_kernel(
    sel_ref, basis_ref, blocks_ref, groups_ref, meta_ref,
    recv_ref, mx_ref, pot_ref,
    phi, wgt, a3, mperm, mat, rho, hr, vpot, kb, table, send, mz, xs,
    load_sem, own_sem, halo_send, halo_recv, mz_send, mz_recv, mx_send, mx_recv, blk_send, blk_recv,
):
    i = lax.axis_index("gx")
    j = lax.axis_index("gy")
    k = lax.axis_index("gz")
    me = i * N + j

    loads = []
    for n in range(NCHUNK):
        cols = pl.ds(n * CHUNK, CHUNK)
        copy = pltpu.make_async_copy(basis_ref.at[:, cols], phi.at[:, cols], load_sem.at[n])
        copy.start()
        loads.append(copy)

    barrier = pltpu.get_barrier_semaphore()

    def greet(t, carry):
        pl.semaphore_signal(
            barrier, inc=1,
            device_id=(lax.rem(i + t // N, N), lax.rem(j + lax.rem(t, N), N), k),
            device_id_type=MESH,
        )
        return carry

    lax.fori_loop(1, OWNERS, greet, 0)
    for a, b, c in OUT_PLANE:
        pl.semaphore_signal(
            barrier, inc=1,
            device_id=(lax.rem(i + a + N, N), lax.rem(j + b + N, N), lax.rem(k + c + N, N)),
            device_id_type=MESH,
        )

    lane = lax.broadcasted_iota(jnp.int32, (ROW_BLK, 128), 1)
    low = lane < BASIS
    r64 = lax.broadcasted_iota(jnp.int32, (BASIS, BASIS), 0)
    c64 = lax.broadcasted_iota(jnp.int32, (BASIS, BASIS), 1)
    split_rows = jnp.where(c64 == 2 * (r64 % 32) + r64 // 32, 1.0, 0.0).astype(BF16)
    join_rows = jnp.where(r64 == 2 * (c64 % 32) + c64 // 32, 1.0, 0.0).astype(BF16)

    codes = groups_ref[0:1, :] * G + groups_ref[1:2, :]
    pick = jnp.where(
        lax.broadcasted_iota(jnp.int32, (CODES, PAIRS), 0) == codes, 1.0, 0.0
    ).astype(BF16)
    for n in range(8):
        part = jnp.dot(pick, blocks_ref[:, n * 512:(n + 1) * 512], preferred_element_type=F32)
        for q in range(4):
            a3[pl.ds(n * 4 + q, CODES, stride=ROW_BLK), :] = part[:, q * 128:(q + 1) * 128]
    for a in range(G):
        for bp in range(4):
            even = a3[(a * G + 2 * bp) * ROW_BLK:(a * G + 2 * bp + 1) * ROW_BLK, :]
            if 2 * bp + 1 < G:
                odd = a3[(a * G + 2 * bp + 1) * ROW_BLK:(a * G + 2 * bp + 2) * ROW_BLK, :]
            else:
                odd = jnp.zeros((ROW_BLK, 128), F32)
            top = jnp.where(low, even, pltpu.roll(odd, 64, axis=1))
            bottom = jnp.where(low, pltpu.roll(even, 64, axis=1), odd)
            mperm[a * 64:a * 64 + 32, bp * 128:(bp + 1) * 128] = top.astype(BF16)
            mperm[a * 64 + 32:(a + 1) * 64, bp * 128:(bp + 1) * 128] = bottom.astype(BF16)
        mat[a * 64:(a + 1) * 64, :] = jnp.dot(
            join_rows, mperm[a * 64:(a + 1) * 64, :], preferred_element_type=F32
        ).astype(BF16)

    for n in range(NCHUNK):
        loads[n].wait()
        cols = slice(n * CHUNK, (n + 1) * CHUNK)
        part = phi[:, cols]
        image = jnp.dot(mat[:, :ROWS], part, preferred_element_type=F32)
        line = jnp.sum(part.astype(F32) * image, axis=0, keepdims=True)
        for q in range(CHUNK // 256):
            x = n * (CHUNK // 256) + q
            rho[x:x + 1, :] = line[:, q * 256:(q + 1) * 256]

    pl.semaphore_wait(barrier, PEERS)

    for n, (a, b, c) in enumerate(DIRS):
        src = rho.at[half(a, pl.ds(0, 8), pl.ds(8, 8), pl.ds(0, 16)),
                     half(b, pl.ds(0, 128), pl.ds(128, 128), pl.ds(0, 256))]
        dst = hr.at[n, half(-a, pl.ds(0, 8), pl.ds(8, 8), pl.ds(0, 16)),
                    half(-b, pl.ds(0, 128), pl.ds(128, 128), pl.ds(0, 256))]
        pltpu.make_async_remote_copy(
            src_ref=src, dst_ref=dst, send_sem=halo_send, recv_sem=halo_recv,
            device_id=(lax.rem(i + a + N, N), lax.rem(j + b + N, N), lax.rem(k + c + N, N)),
            device_id_type=MESH,
        ).start()

    def send_z(t, carry):
        ti = lax.rem(i + t, N)
        pltpu.make_async_remote_copy(
            src_ref=meta_ref.at[ti], dst_ref=mz.at[i], send_sem=mz_send, recv_sem=mz_recv,
            device_id=(ti, j, k), device_id_type=MESH,
        ).start()
        return carry

    lax.fori_loop(1, N, send_z, 0)
    mz[i] = meta_ref[i]

    bytes_wait(hr.at[0:11], halo_recv)
    zlow = lax.rem(lax.broadcasted_iota(jnp.int32, (8, 128), 1), EXT) < 8
    for hx in range(2):
        for hy in range(2):
            rows = slice(hx * 8, hx * 8 + 8)
            cols = slice(hy * 128, hy * 128 + 128)
            total = rho[rows, cols]
            steps_x = (0, 1 - 2 * hx)
            steps_y = (0, 1 - 2 * hy)
            for a in steps_x:
                for b in steps_y:
                    if (a, b) != (0, 0):
                        total = total + hr[DIR_ID[(a, b, 0)], rows, cols]
            sides = []
            for c in (1, -1):
                side = None
                for a in steps_x:
                    for b in steps_y:
                        term = hr[DIR_ID[(a, b, c)], rows, cols]
                        side = term if side is None else side + term
                sides.append(side)
            total = total + jnp.where(
                zlow, pltpu.roll(sides[0], 120, axis=1), pltpu.roll(sides[1], 8, axis=1)
            )
            cubic = jnp.exp(jnp.log(total * total + 1.0) * (-1.0 / 3.0))
            vpot[rows, cols] = -XC_COEF * total * cubic
    left = vpot[4:12, 0:128]
    right = vpot[4:12, 128:256]
    lane8 = lax.broadcasted_iota(jnp.int32, (8, 128), 1)
    pot_ref[...] = jnp.where(
        lane8 < 64, pltpu.roll(left, 64, axis=1), pltpu.roll(right, 64, axis=1)
    )

    bytes_wait(mz.at[0:N - 1], mz_recv)
    for t in range(N):
        xs[t] = mz[:, t, :]

    def send_x(t, carry):
        tj = lax.rem(j + t, N)
        pltpu.make_async_remote_copy(
            src_ref=xs.at[tj], dst_ref=mx_ref.at[j], send_sem=mx_send, recv_sem=mx_recv,
            device_id=(i, tj, k), device_id_type=MESH,
        ).start()
        return carry

    lax.fori_loop(1, N, send_x, 0)
    own_meta = pltpu.make_async_copy(xs.at[j], mx_ref.at[j], own_sem.at[0])
    own_meta.start()

    for x in range(EXT):
        cols = slice(x * 256, (x + 1) * 256)
        wgt[:, cols] = (phi[:, cols].astype(F32) * vpot[x:x + 1, :]).astype(BF16)
    ks = lax.dot_general(
        wgt[...], phi[...], (((1,), (1,)), ((), ())), preferred_element_type=F32
    )
    kb[:, 0:ROWS] = (ks * GRID_WEIGHT).astype(BF16)
    kb[:, ROWS:] = jnp.zeros((ROWS, WIDE - ROWS), BF16)
    for a in range(G):
        rows = jnp.dot(split_rows, kb[a * 64:(a + 1) * 64, :], preferred_element_type=F32)
        for bp in range(4):
            top = rows[0:32, bp * 128:(bp + 1) * 128]
            bottom = rows[32:64, bp * 128:(bp + 1) * 128]
            table[a * G + 2 * bp] = jnp.where(low, top, pltpu.roll(bottom, 64, axis=1)).astype(BF16)
            if 2 * bp + 1 < G:
                table[a * G + 2 * bp + 1] = jnp.where(
                    low, pltpu.roll(top, 64, axis=1), bottom
                ).astype(BF16)

    def pack(target):
        send[target, 0] = table[sel_ref[target]]
        send[target, 1] = table[sel_ref[OWNERS + target]]

    for di in FAR_FIRST:
        ti = lax.rem(i + di, N)

        def send_block(t, carry, ti=ti):
            tj = lax.rem(j + t, N)
            target = ti * N + tj
            pack(target)
            pltpu.make_async_remote_copy(
                src_ref=send.at[target], dst_ref=recv_ref.at[me], send_sem=blk_send,
                recv_sem=blk_recv, device_id=(ti, tj, k), device_id_type=MESH,
            ).start()
            return carry

        lax.fori_loop(0 if di else 1, N, send_block, 0)
    pack(me)
    own = pltpu.make_async_copy(send.at[me], recv_ref.at[me], own_sem.at[1])
    own.start()

    own.wait()
    own_meta.wait()
    bytes_wait(xs.at[0:N - 1], mx_send)
    bytes_wait(mz.at[0:N - 1], mz_send)
    bytes_wait(hr.at[0:11], halo_send)
    bytes_wait(mx_ref.at[0:N - 1], mx_recv)
    bytes_wait(send.at[0:OWNERS - 1], blk_send)
    bytes_wait(recv_ref.at[0:OWNERS - 1], blk_recv)


def store_kernel(mx_ref, recv_ref, out_ref, acc):
    acc[...] = jnp.zeros_like(acc)

    def add(t, carry):
        row = (t % N) * N + t // N
        for rank in range(2):
            slot = mx_ref[row, rank * 64]
            slot = jnp.where(slot < 0, PAIRS, slot)
            at = pl.ds(pl.multiple_of(slot * ROW_BLK, ROW_BLK), ROW_BLK)
            acc[at, :] += recv_ref[t, rank].astype(F32)
        return carry

    lax.fori_loop(0, OWNERS, add, 0)
    for c in range(ROW_BLK):
        out_ref[:, c * 128:(c + 1) * 128] = acc[pl.ds(c, PAIRS, stride=ROW_BLK), :].astype(BF16)


def per_device(basis, density_blocks, pair_groups, owner, owner_slot):
    codes = pair_groups[0] * G + pair_groups[1]
    names = owner[:, 0]
    order = jnp.arange(PAIRS, dtype=jnp.int32)
    earlier = (names[:, None] == names[None, :]) & (order[:, None] > order[None, :])
    rank = jnp.sum(earlier.astype(jnp.int32), axis=1)
    place = rank * OWNERS + names
    match = jnp.arange(2 * OWNERS, dtype=jnp.int32)[:, None] == place[None, :]
    sel = jnp.sum(jnp.where(match, codes[None, :], 0), axis=1)
    slots = jnp.sum(jnp.where(match, owner_slot[None, :] + 1, 0), axis=1) - 1
    meta = jnp.broadcast_to(slots.reshape(2, N, N, 1), (2, N, N, 64))
    meta = jnp.concatenate([meta[0], meta[1]], axis=-1)

    vmem = pl.BlockSpec(memory_space=pltpu.VMEM)
    smem = pl.BlockSpec(memory_space=pltpu.SMEM)
    hbm = pl.BlockSpec(memory_space=pl.ANY)
    recv, mx, pot = pl.pallas_call(
        main_kernel,
        name="collocate_exchange",
        out_shape=(
            jax.ShapeDtypeStruct((OWNERS, 2, ROW_BLK, 128), BF16),
            jax.ShapeDtypeStruct((N, N, 128), jnp.int32),
            jax.ShapeDtypeStruct((8, 128), F32),
        ),
        in_specs=[smem, hbm, vmem, vmem, vmem],
        out_specs=(hbm, hbm, vmem),
        scratch_shapes=[
            pltpu.VMEM((ROWS, EXT3), BF16),
            pltpu.VMEM((ROWS, EXT3), BF16),
            pltpu.VMEM((CODES * ROW_BLK, 128), F32),
            pltpu.VMEM((ROWS, WIDE), BF16),
            pltpu.VMEM((ROWS, WIDE), BF16),
            pltpu.VMEM((EXT, 256), F32),
            pltpu.VMEM((len(DIRS), EXT, 256), F32),
            pltpu.VMEM((EXT, 256), F32),
            pltpu.VMEM((ROWS, WIDE), BF16),
            pltpu.VMEM((G * G, ROW_BLK, 128), BF16),
            pltpu.VMEM((OWNERS, 2, ROW_BLK, 128), BF16),
            pltpu.VMEM((N, N, 128), jnp.int32),
            pltpu.VMEM((N, N, 128), jnp.int32),
            pltpu.SemaphoreType.DMA((NCHUNK,)),
            pltpu.SemaphoreType.DMA((2,)),
        ] + [pltpu.SemaphoreType.DMA] * 8,
        compiler_params=pltpu.CompilerParams(
            collective_id=1, has_side_effects=True, vmem_limit_bytes=40 << 20
        ),
        cost_estimate=pl.CostEstimate(
            flops=4 * ROWS * ROWS * EXT3, bytes_accessed=6 << 20, transcendentals=2 * EXT3
        ),
    )(sel, basis.reshape(ROWS, EXT3), density_blocks, pair_groups, meta)

    ks_blocks = pl.pallas_call(
        store_kernel,
        name="store_blocks",
        out_shape=jax.ShapeDtypeStruct((PAIRS, 4096), BF16),
        in_specs=[smem, vmem],
        out_specs=vmem,
        scratch_shapes=[pltpu.VMEM(((PAIRS + 1) * ROW_BLK, 128), F32)],
        compiler_params=pltpu.CompilerParams(vmem_limit_bytes=32 << 20),
    )(mx.reshape(N * N, 128), recv)
    potential = pot.reshape(8, 8, EXT)[:, :, RIM:RIM + 8]
    return ks_blocks, potential


def solution(mesh):
    return jax.shard_map(
        per_device,
        mesh=mesh,
        in_specs=(
            P(("gx", "gy", "gz"), None, None),
            P(("gx", "gy", "gz"), None),
            P(None, ("gx", "gy", "gz")),
            P(("gx", "gy", "gz"), None),
            P(("gx", "gy", "gz")),
        ),
        out_specs=(P(("gx", "gy", "gz"), None), P("gx", "gy", "gz")),
        check_vma=False,
    )
```

time: 122 us -> 63.7 us (0.52)
  the two profiles are of different devices: /device:TPU:16 before, /device:TPU:1 now
where the time goes in v1:
time: 63.7 us; the launch traced here: 63.4 us
  Pallas kernels  55.3 us (87%)
  local copies, waits for them, and re-layouts  4.86 us (8%)
  other arithmetic  2.54 us (4%)
  between operations  0.66 us (1%)
    pallas_call x1, Pallas kernels, per_device(): pl.pallas_call(main_kernel, name='collocate_exchange', out_shape=(jax.Sha...  51.7 us
    unnamed x6, local copies, waits for them, and re-layouts  3.72 us
    pallas_call x1, Pallas kernels, per_device(): pl.pallas_call(store_kernel, name='store_blocks', out_shape=jax.ShapeDtyp...  3.65 us

profile of v1, /device:TPU:1, one launch (start us, length us, event | category | flops | bytes accessed | tf_op | source)
XLA Modules:
  0.0 63.4 jit_solution(14201274426669767742)
XLA Ops:
  0.6 0.9 %convert_reduce_fusion = s32[48]{0:T(128)S(1)} fusion(s32[48]{0:T(128)} %bitcast.8), kind=kLoop, calls=%fused_computation.3 | loop fusion | flops 11472 | bytes 384 | tf_op jit(solution)/shard_map/reduce_sum | solution.py:268
  1.5 0.8 %add_bitcast_fusion = s32[48]{0:T(128)S(1)} fusion(s32[2,48]{1,0:T(2,128)} %groups_ref.1), kind=kLoop, calls=%fused_computation.7 | loop fusion | flops 96 | bytes 576 | tf_op jit(solution)/shard_map/jit(_where)/broadcast_in_dim | solution.py:271
  2.3 0.7 %multiply_add_fusion = (s32[48]{0:T(128)S(1)}, s32[48]{0:T(128)S(1)}) fusion(s32[48]{0:T(128)S(1)} %convert_reduce_fusion, s32[48,1]{0,1:T(1,128)} %param.8, s32[48]{0:T(128)} %param.9), kind=kLoop, calls=%fused_computation.8 | loop fusion | flops 144 | bytes 960 | tf_op jit(solution)/shard_map/add | solution.py:269
  3.0 0.1 select_reduce_fusion
  3.1 0.1 fusion.1
  3.2 0.1 broadcast_in_dim.41
  3.2 0.1 broadcast_in_dim.43
  3.3 0.1 broadcast_in_dim.44
  3.4 0.1 broadcast_in_dim.42
  3.5 0.1 pad_add_fusion.meta_ref
  3.6 0.0 copy-start
  3.6 2.0 %copy-done = bf16[7,64,4096]{2,1,0:T(8,128)(2,1)S(1)} copy-done((bf16[7,64,4096]{2,1,0:T(8,128)(2,1)S(1)}, bf16[7,64,4096]{2,1,0:T(8,128)(2,1)}, u32[]{:S(2)}) %copy-start) | copy-done | bytes 3670040
  5.6 0.0 copy-start.1
  5.6 1.0 %copy-done.1 = bf16[48,4096]{1,0:T(8,128)(2,1)S(1)} copy-done((bf16[48,4096]{1,0:T(8,128)(2,1)S(1)}, bf16[48,4096]{1,0:T(8,128)(2,1)}, u32[]{:S(2)}) %copy-start.1) | copy-done | bytes 393240
  6.6 0.0 copy-start.2
  6.6 0.7 %copy-done.2 = s32[2,48]{1,0:T(2,128)S(1)} copy-done((s32[2,48]{1,0:T(2,128)S(1)}, s32[2,48]{1,0:T(2,128)}, u32[]{:S(2)}) %copy-start.2) | copy-done | bytes 408
  7.3 51.7 %collocate_exchange.1 = (bf16[64,2,32,128]{3,2,1,0:T(8,128)(2,1)S(1)}, s32[8,8,128]{2,1,0:T(8,128)S(1)}, f32[8,128]{1,0:T(8,128)S(1)}) custom-call(s32[128]{0:T(128)S(1)} %get-tuple-element.9.sel_ref, bf16[448,4096]{1,0:T(8,128)(2,1)S(1)} %bitcast.7, bf16[48,4096]{1,0:T(8,128)(2,1)S(1)} %copy-done.1, s32[2,48]{1,0:T(2,128)S(1)} %copy-done.2, ...), custom_call_target="tpu_custom_call" | custom-call | flops 3288334336 | bytes 6291456 | tf_op jit(solution)/shard_map/collocate_exchange/pallas_call | solution.py:279
  59.0 3.6 %store_blocks.1 = bf16[48,4096]{1,0:T(8,128)(2,1)} custom-call(s32[64,128]{1,0:T(8,128)S(1)} %bitcast.6, bf16[64,2,32,128]{3,2,1,0:T(8,128)(2,1)S(1)} %get-tuple-element.6.recv_ref), custom_call_target="tpu_custom_call" | custom-call | tf_op jit(solution)/shard_map/store_blocks/pallas_call | solution.py:314
  62.6 0.1 reshape.49
  62.7 0.7 %slice.26 = f32[8,8,8]{2,1,0:T(8,128)} slice(f32[8,8,16]{2,1,0:T(8,128)S(1)} %reshape.49), slice={[0:8], [0:8], [4:12]} | slice | bytes 4096 | tf_op jit(solution)/shard_map/slice | solution.py:323
  (1 shorter events, 0.0 us)
Async XLA Ops:
  3.6 2.0 %copy-start = (bf16[7,64,4096]{2,1,0:T(8,128)(2,1)S(1)}, bf16[7,64,4096]{2,1,0:T(8,128)(2,1)}, u32[]{:S(2)}) copy-start(bf16[7,64,4096]{2,1,0:T(8,128)(2,1)} %param.5) | copy-start | bytes 11010052
  5.6 1.0 %copy-start.1 = (bf16[48,4096]{1,0:T(8,128)(2,1)S(1)}, bf16[48,4096]{1,0:T(8,128)(2,1)}, u32[]{:S(2)}) copy-start(bf16[48,4096]{1,0:T(8,128)(2,1)} %blocks_ref.1) | copy-start | bytes 1179652
  6.6 0.7 %copy-start.2 = (s32[2,48]{1,0:T(2,128)S(1)}, s32[2,48]{1,0:T(2,128)}, u32[]{:S(2)}) copy-start(s32[2,48]{1,0:T(2,128)} %groups_ref.1) | copy-start | bytes 1156

commit v2 on v1

--- a/solution.py
+++ b/solution.py
@@ -31,8 +31,12 @@
 DIRS = [(a, b, c) for c in (0, 1, -1) for a in (0, 1, -1) for b in (0, 1, -1) if (a, b, c) != (0, 0, 0)]
 DIR_ID = {d: n for n, d in enumerate(DIRS)}
 OUT_PLANE = [d for d in DIRS if d[2] != 0]
-PEERS = OWNERS - 1 + len(OUT_PLANE)
+FAR_Z = (2, 3, 4, 5, 6)
+PEERS = OWNERS - 1 + len(OUT_PLANE) + len(FAR_Z)
 FAR_FIRST = (4, 3, 5, 2, 6, 1, 7, 0)
+SECOND = 3
+PARTS = 4
+FLAG = 128
 
 
 def half(step, low, high, whole):
@@ -44,16 +48,23 @@
 
 
 def main_kernel(
-    sel_ref, basis_ref, blocks_ref, groups_ref, meta_ref,
-    recv_ref, mx_ref, pot_ref,
-    phi, wgt, a3, mperm, mat, rho, hr, vpot, kb, table, send, mz, xs,
+    basis_ref, blocks_ref, groups_ref, owner_ref, slot_ref,
+    recv_ref, recv2_ref, slots_out, flag_out, pot_ref, table_ref,
+    phi, wgt, blk, gv, ov, sv, a3, mperm, mat, rho, hr, vpot, kb, table, send, z2s, z2r, x2s,
+    selv, sels, meta, mz, xs, mx, fl, fr, potv, slotv,
     load_sem, own_sem, halo_send, halo_recv, mz_send, mz_recv, mx_send, mx_recv, blk_send, blk_recv,
+    z2_send, z2_recv, x2_send, x2_recv, fl_send, fl_recv,
 ):
     i = lax.axis_index("gx")
     j = lax.axis_index("gy")
     k = lax.axis_index("gz")
     me = i * N + j
 
+    small = []
+    for n, (src, dst) in enumerate(((groups_ref, gv), (owner_ref, ov), (slot_ref, sv), (blocks_ref, blk))):
+        copy = pltpu.make_async_copy(src, dst, load_sem.at[NCHUNK + n])
+        copy.start()
+        small.append(copy)
     loads = []
     for n in range(NCHUNK):
         cols = pl.ds(n * CHUNK, CHUNK)
@@ -72,7 +83,7 @@
         return carry
 
     lax.fori_loop(1, OWNERS, greet, 0)
-    for a, b, c in OUT_PLANE:
+    for a, b, c in OUT_PLANE + [(0, 0, t) for t in FAR_Z]:
         pl.semaphore_signal(
             barrier, inc=1,
             device_id=(lax.rem(i + a + N, N), lax.rem(j + b + N, N), lax.rem(k + c + N, N)),
@@ -86,12 +97,59 @@
     split_rows = jnp.where(c64 == 2 * (r64 % 32) + r64 // 32, 1.0, 0.0).astype(BF16)
     join_rows = jnp.where(r64 == 2 * (c64 % 32) + c64 // 32, 1.0, 0.0).astype(BF16)
 
-    codes = groups_ref[0:1, :] * G + groups_ref[1:2, :]
+    for copy in small[:3]:
+        copy.wait()
+    row = lax.broadcasted_iota(jnp.int32, (PAIRS, PAIRS), 0)
+    col = lax.broadcasted_iota(jnp.int32, (PAIRS, PAIRS), 1)
+
+    def upright(line):
+        return jnp.sum(jnp.where(row == col, line, 0), axis=1, keepdims=True)
+
+    def count(mask, axis):
+        return jnp.sum(jnp.where(mask, 1, 0), axis=axis, keepdims=True)
+
+    codes = gv[0:1, :] * G + gv[1:2, :]
+    own_r = ov[...]
+    own_c = upright(own_r)
+    code_c = upright(codes)
+    grp_r = own_r // N
+    grp_c = own_c // N
+    same = own_c == own_r
+    rank_c = count(same & (col < row), 1)
+    rank_r = count(same & (row < col), 0)
+    mates = grp_c == grp_r
+    idx_c = count(mates & (own_r < own_c) & (rank_r > 0), 1)
+    idx_r = count(mates & (own_c < own_r) & (rank_c > 0), 0)
+    place_c = rank_c * OWNERS + own_c
+    place_r = rank_r * OWNERS + own_r
+    wide = lax.broadcasted_iota(jnp.int32, (PAIRS, 128), 1)
+    sel1 = jnp.sum(jnp.where(wide == place_c, code_c, 0), axis=0, keepdims=True)
+    second_at = jnp.where((rank_c > 0) & (idx_c < SECOND), grp_c * SECOND + idx_c, -1)
+    sel2 = jnp.sum(jnp.where(wide == second_at, code_c, 0), axis=0, keepdims=True)
+    selv[0:1, :] = sel1
+    selv[1:2, :] = sel2
+    sel_copy = pltpu.make_async_copy(selv, sels, own_sem.at[0])
+    sel_copy.start()
+    tall = lax.broadcasted_iota(jnp.int32, (OWNERS, PAIRS), 0)
+    first_m = tall == place_r
+    second_m = tall + OWNERS == place_r
+    first_slot = jnp.sum(jnp.where(first_m, sv[...] + 1, 0), axis=1, keepdims=True) - 1
+    second_slot = jnp.sum(jnp.where(second_m, sv[...] + 1, 0), axis=1, keepdims=True) - 1
+    second_idx = jnp.sum(jnp.where(second_m, idx_r + 1, 0), axis=1, keepdims=True) - 1
+    over = jnp.max(jnp.where((rank_r > 0) & (idx_r >= SECOND), FLAG, 0), axis=1, keepdims=True)
+    wide64 = lax.broadcasted_iota(jnp.int32, (OWNERS, 128), 1)
+    tile = jnp.where(wide64 < OWNERS, first_slot + over, second_slot)
+    index = jnp.broadcast_to(second_idx, (OWNERS, 128))
+    for t in range(N):
+        meta[t, 0] = tile[t * N:(t + 1) * N]
+        meta[t, 1] = index[t * N:(t + 1) * N]
+
     pick = jnp.where(
         lax.broadcasted_iota(jnp.int32, (CODES, PAIRS), 0) == codes, 1.0, 0.0
     ).astype(BF16)
+    small[3].wait()
     for n in range(8):
-        part = jnp.dot(pick, blocks_ref[:, n * 512:(n + 1) * 512], preferred_element_type=F32)
+        part = jnp.dot(pick, blk[:, n * 512:(n + 1) * 512], preferred_element_type=F32)
         for q in range(4):
             a3[pl.ds(n * 4 + q, CODES, stride=ROW_BLK), :] = part[:, q * 128:(q + 1) * 128]
     for a in range(G):
@@ -135,13 +193,13 @@
     def send_z(t, carry):
         ti = lax.rem(i + t, N)
         pltpu.make_async_remote_copy(
-            src_ref=meta_ref.at[ti], dst_ref=mz.at[i], send_sem=mz_send, recv_sem=mz_recv,
+            src_ref=meta.at[ti], dst_ref=mz.at[i], send_sem=mz_send, recv_sem=mz_recv,
             device_id=(ti, j, k), device_id_type=MESH,
         ).start()
         return carry
 
     lax.fori_loop(1, N, send_z, 0)
-    mz[i] = meta_ref[i]
+    mz[i] = meta[i]
 
     bytes_wait(hr.at[0:11], halo_recv)
     zlow = lax.rem(lax.broadcasted_iota(jnp.int32, (8, 128), 1), EXT) < 8
@@ -172,25 +230,26 @@
     left = vpot[4:12, 0:128]
     right = vpot[4:12, 128:256]
     lane8 = lax.broadcasted_iota(jnp.int32, (8, 128), 1)
-    pot_ref[...] = jnp.where(
+    potv[...] = jnp.where(
         lane8 < 64, pltpu.roll(left, 64, axis=1), pltpu.roll(right, 64, axis=1)
     )
+    pot_copy = pltpu.make_async_copy(potv, pot_ref, own_sem.at[3])
+    pot_copy.start()
 
     bytes_wait(mz.at[0:N - 1], mz_recv)
     for t in range(N):
-        xs[t] = mz[:, t, :]
+        xs[t] = mz[:, 0, t, :]
 
     def send_x(t, carry):
         tj = lax.rem(j + t, N)
         pltpu.make_async_remote_copy(
-            src_ref=xs.at[tj], dst_ref=mx_ref.at[j], send_sem=mx_send, recv_sem=mx_recv,
+            src_ref=xs.at[tj], dst_ref=mx.at[j], send_sem=mx_send, recv_sem=mx_recv,
             device_id=(i, tj, k), device_id_type=MESH,
         ).start()
         return carry
 
     lax.fori_loop(1, N, send_x, 0)
-    own_meta = pltpu.make_async_copy(xs.at[j], mx_ref.at[j], own_sem.at[0])
-    own_meta.start()
+    mx[j] = xs[j]
 
     for x in range(EXT):
         cols = slice(x * 256, (x + 1) * 256)
@@ -211,9 +270,27 @@
                     low, pltpu.roll(top, 64, axis=1), bottom
                 ).astype(BF16)
 
-    def pack(target):
-        send[target, 0] = table[sel_ref[target]]
-        send[target, 1] = table[sel_ref[OWNERS + target]]
+    sel_copy.wait()
+    keep = pltpu.make_async_copy(table, table_ref, own_sem.at[0])
+    keep.start()
+
+    def pack_second(t, carry):
+        for c in range(SECOND):
+            z2s[t, c] = table[sels[1, t * SECOND + c]]
+        return carry
+
+    lax.fori_loop(0, N, pack_second, 0)
+
+    def send_second(t, carry):
+        ti = lax.rem(i + t, N)
+        pltpu.make_async_remote_copy(
+            src_ref=z2s.at[ti], dst_ref=z2r.at[i], send_sem=z2_send, recv_sem=z2_recv,
+            device_id=(ti, j, k), device_id_type=MESH,
+        ).start()
+        return carry
+
+    lax.fori_loop(1, N, send_second, 0)
+    z2r[i] = z2s[i]
 
     for di in FAR_FIRST:
         ti = lax.rem(i + di, N)
@@ -221,7 +298,7 @@
         def send_block(t, carry, ti=ti):
             tj = lax.rem(j + t, N)
             target = ti * N + tj
-            pack(target)
+            send[target] = table[sels[0, target]]
             pltpu.make_async_remote_copy(
                 src_ref=send.at[target], dst_ref=recv_ref.at[me], send_sem=blk_send,
                 recv_sem=blk_recv, device_id=(ti, tj, k), device_id_type=MESH,
@@ -229,66 +306,200 @@
             return carry
 
         lax.fori_loop(0 if di else 1, N, send_block, 0)
-    pack(me)
+    send[me] = table[sels[0, me]]
     own = pltpu.make_async_copy(send.at[me], recv_ref.at[me], own_sem.at[1])
     own.start()
 
+    bytes_wait(mx.at[0:N - 1], mx_recv)
+    wide8 = lax.broadcasted_iota(jnp.int32, (N, 128), 1)
+    sub8 = lax.broadcasted_iota(jnp.int32, (N, 128), 0)
+    slots = jnp.zeros((N, 128), jnp.int32)
+    over = jnp.zeros((N, 128), jnp.int32)
+    for t in range(N):
+        part = mx[t]
+        left_over = (wide8 < OWNERS) & (part >= FLAG - 1)
+        over = jnp.maximum(over, jnp.where(left_over, 1, 0))
+        value = jnp.where(left_over, part - FLAG, part)
+        here = (wide8 == sub8 * N + t) | (wide8 == OWNERS + t * N + sub8)
+        slots = slots + jnp.where(here, value, 0)
+    slotv[...] = jnp.broadcast_to(jnp.sum(slots, axis=0, keepdims=True), (N, 128))
+    slot_copy = pltpu.make_async_copy(slotv, slots_out, own_sem.at[4])
+    slot_copy.start()
+    fl[...] = over
+
+    def send_flag(t, carry):
+        tk = lax.rem(k + t, N)
+        pltpu.make_async_remote_copy(
+            src_ref=fl, dst_ref=fr.at[k], send_sem=fl_send, recv_sem=fl_recv,
+            device_id=(i, j, tk), device_id_type=MESH,
+        ).start()
+        return carry
+
+    lax.fori_loop(1, N, send_flag, 0)
+    fr[k] = over
+
+    bytes_wait(z2r.at[0:N - 1], z2_recv)
+    for t in range(N):
+        def place_second(a, carry, t=t):
+            index = jnp.broadcast_to(mz[a, 1, t:t + 1, :], (ROW_BLK, 128))
+            total = jnp.zeros((ROW_BLK, 128), F32)
+            for c in range(SECOND):
+                total = jnp.where(index == c, z2r[a, c].astype(F32), total)
+            x2s[t, a] = total.astype(BF16)
+            return carry
+
+        lax.fori_loop(0, N, place_second, 0)
+
+    def forward(t, carry):
+        tj = lax.rem(j + t, N)
+        pltpu.make_async_remote_copy(
+            src_ref=x2s.at[tj], dst_ref=recv2_ref.at[j], send_sem=x2_send, recv_sem=x2_recv,
+            device_id=(i, tj, k), device_id_type=MESH,
+        ).start()
+        return carry
+
+    lax.fori_loop(1, N, forward, 0)
+    own2 = pltpu.make_async_copy(x2s.at[j], recv2_ref.at[j], own_sem.at[2])
+    own2.start()
+
+    bytes_wait(fr.at[0:N - 1], fl_recv)
+    for t in range(N):
+        over = jnp.maximum(over, fr[t])
+    flag_out[...] = jnp.max(jnp.max(over, axis=0, keepdims=True), axis=1, keepdims=True)
+
+    for copy in (keep, pot_copy, slot_copy):
+        copy.wait()
     own.wait()
-    own_meta.wait()
+    own2.wait()
+    bytes_wait(fr.at[0:N - 1], fl_send)
     bytes_wait(xs.at[0:N - 1], mx_send)
     bytes_wait(mz.at[0:N - 1], mz_send)
     bytes_wait(hr.at[0:11], halo_send)
-    bytes_wait(mx_ref.at[0:N - 1], mx_recv)
+    bytes_wait(z2s.at[0:N - 1], z2_send)
+    bytes_wait(x2s.at[0:N - 1], x2_send)
     bytes_wait(send.at[0:OWNERS - 1], blk_send)
+    bytes_wait(recv2_ref.at[0:N - 1], x2_recv)
     bytes_wait(recv_ref.at[0:OWNERS - 1], blk_recv)
 
 
-def store_kernel(mx_ref, recv_ref, out_ref, acc):
+def store_kernel(
+    slots_ref, recv_ref, recv2_ref, pot_ref, out_ref, pot_out,
+    acc, slots, got, got2, pot, cells, rows, sem, out_sem,
+):
+    def start(src, dst, at):
+        copy = pltpu.make_async_copy(src, dst, at)
+        copy.start()
+        return copy
+
+    few = OWNERS // PARTS
+    slots_in = start(slots_ref, slots, sem.at[2 * PARTS])
+    pot_in = start(pot_ref, pot, sem.at[2 * PARTS + 1])
+    parts = []
+    for n in range(PARTS):
+        part = pl.ds(n * few, few)
+        parts.append((
+            start(recv_ref.at[part], got.at[part], sem.at[2 * n]),
+            start(recv2_ref.at[part], got2.at[part], sem.at[2 * n + 1]),
+        ))
     acc[...] = jnp.zeros_like(acc)
+    pot_in.wait()
+    for y in range(8):
+        cells[:, y, :] = pot[:, y * EXT + RIM:y * EXT + RIM + 8]
+    outs = [start(cells, pot_out, out_sem.at[PARTS])]
 
     def add(t, carry):
-        row = (t % N) * N + t // N
-        for rank in range(2):
-            slot = mx_ref[row, rank * 64]
+        for rank, ref in enumerate((got, got2)):
+            slot = slots[0, rank * OWNERS + t]
             slot = jnp.where(slot < 0, PAIRS, slot)
             at = pl.ds(pl.multiple_of(slot * ROW_BLK, ROW_BLK), ROW_BLK)
-            acc[at, :] += recv_ref[t, rank].astype(F32)
-        return carry
-
-    lax.fori_loop(0, OWNERS, add, 0)
-    for c in range(ROW_BLK):
-        out_ref[:, c * 128:(c + 1) * 128] = acc[pl.ds(c, PAIRS, stride=ROW_BLK), :].astype(BF16)
-
-
-def per_device(basis, density_blocks, pair_groups, owner, owner_slot):
+            acc[at, :] += ref[t].astype(F32)
+        return carry
+
+    slots_in.wait()
+    for n in range(PARTS):
+        for copy in parts[n]:
+            copy.wait()
+        lax.fori_loop(n * few, (n + 1) * few, add, 0, unroll=4)
+    wide = ROW_BLK // PARTS
+    for n in range(PARTS):
+        for c in range(n * wide, (n + 1) * wide):
+            rows[:, c * 128:(c + 1) * 128] = acc[pl.ds(c, PAIRS, stride=ROW_BLK), :].astype(BF16)
+        cols = pl.ds(n * wide * 128, wide * 128)
+        outs.append(start(rows.at[:, cols], out_ref.at[:, cols], out_sem.at[n]))
+    for copy in outs:
+        copy.wait()
+
+
+def store(slots, recv, recv2, pot):
+    hbm = pl.BlockSpec(memory_space=pl.ANY)
+    return pl.pallas_call(
+        store_kernel,
+        name="store_blocks",
+        out_shape=(
+            jax.ShapeDtypeStruct((PAIRS, 4096), BF16),
+            jax.ShapeDtypeStruct((8, 8, 8), F32),
+        ),
+        in_specs=[hbm] * 4,
+        out_specs=(hbm, hbm),
+        scratch_shapes=[
+            pltpu.VMEM(((PAIRS + 1) * ROW_BLK, 128), F32),
+            pltpu.SMEM((8, 128), jnp.int32),
+            pltpu.VMEM((OWNERS, ROW_BLK, 128), BF16),
+            pltpu.VMEM((OWNERS, ROW_BLK, 128), BF16),
+            pltpu.VMEM((8, 128), F32),
+            pltpu.VMEM((8, 8, 8), F32),
+            pltpu.VMEM((PAIRS, 4096), BF16),
+            pltpu.SemaphoreType.DMA((2 * PARTS + 2,)),
+            pltpu.SemaphoreType.DMA((PARTS + 1,)),
+        ],
+        compiler_params=pltpu.CompilerParams(vmem_limit_bytes=61 << 20),
+    )(slots, recv, recv2, pot)
+
+
+def resend(pair_groups, owner, owner_slot, table, slots, recv, recv2, pot):
     codes = pair_groups[0] * G + pair_groups[1]
     names = owner[:, 0]
     order = jnp.arange(PAIRS, dtype=jnp.int32)
     earlier = (names[:, None] == names[None, :]) & (order[:, None] > order[None, :])
     rank = jnp.sum(earlier.astype(jnp.int32), axis=1)
-    place = rank * OWNERS + names
-    match = jnp.arange(2 * OWNERS, dtype=jnp.int32)[:, None] == place[None, :]
-    sel = jnp.sum(jnp.where(match, codes[None, :], 0), axis=1)
-    slots = jnp.sum(jnp.where(match, owner_slot[None, :] + 1, 0), axis=1) - 1
-    meta = jnp.broadcast_to(slots.reshape(2, N, N, 1), (2, N, N, 64))
-    meta = jnp.concatenate([meta[0], meta[1]], axis=-1)
-
+    match = (jnp.arange(OWNERS, dtype=jnp.int32)[:, None] == names[None, :]) & (rank[None, :] == 1)
+    pick = jnp.sum(jnp.where(match, codes[None, :], 0), axis=1)
+    second = jnp.sum(jnp.where(match, owner_slot[None, :] + 1, 0), axis=1) - 1
+    chosen = (jnp.arange(G * G, dtype=jnp.int32)[None, :] == pick[:, None]).astype(BF16)
+    blocks = lax.dot_general(
+        chosen, table, (((1,), (0,)), ((), ())), preferred_element_type=F32
+    ).astype(BF16)
+    got = lax.all_to_all(blocks, ("gx", "gy"), split_axis=0, concat_axis=0, tiled=True)
+    got_slots = lax.all_to_all(second, ("gx", "gy"), split_axis=0, concat_axis=0, tiled=True)
+    new = jnp.concatenate([slots[:, :OWNERS], jnp.broadcast_to(got_slots[None], (N, OWNERS))], axis=1)
+    return store(new, recv, got, pot)
+
+
+def per_device(basis, density_blocks, pair_groups, owner, owner_slot):
     vmem = pl.BlockSpec(memory_space=pltpu.VMEM)
-    smem = pl.BlockSpec(memory_space=pltpu.SMEM)
     hbm = pl.BlockSpec(memory_space=pl.ANY)
-    recv, mx, pot = pl.pallas_call(
+    block = (ROW_BLK, 128)
+    dma = pltpu.SemaphoreType.DMA
+    recv, recv2, slots, flag, pot, table = pl.pallas_call(
         main_kernel,
         name="collocate_exchange",
         out_shape=(
-            jax.ShapeDtypeStruct((OWNERS, 2, ROW_BLK, 128), BF16),
-            jax.ShapeDtypeStruct((N, N, 128), jnp.int32),
+            jax.ShapeDtypeStruct((OWNERS, *block), BF16),
+            jax.ShapeDtypeStruct((N, N, *block), BF16),
+            jax.ShapeDtypeStruct((N, 128), jnp.int32),
+            jax.ShapeDtypeStruct((1, 1), jnp.int32),
             jax.ShapeDtypeStruct((8, 128), F32),
+            jax.ShapeDtypeStruct((G * G, *block), BF16),
         ),
-        in_specs=[smem, hbm, vmem, vmem, vmem],
-        out_specs=(hbm, hbm, vmem),
+        in_specs=[hbm] * 5,
+        out_specs=(hbm, hbm, hbm, vmem, hbm, hbm),
         scratch_shapes=[
             pltpu.VMEM((ROWS, EXT3), BF16),
             pltpu.VMEM((ROWS, EXT3), BF16),
+            pltpu.VMEM((PAIRS, 4096), BF16),
+            pltpu.VMEM((2, PAIRS), jnp.int32),
+            pltpu.VMEM((1, PAIRS), jnp.int32),
+            pltpu.VMEM((1, PAIRS), jnp.int32),
             pltpu.VMEM((CODES * ROW_BLK, 128), F32),
             pltpu.VMEM((ROWS, WIDE), BF16),
             pltpu.VMEM((ROWS, WIDE), BF16),
@@ -296,32 +507,40 @@
             pltpu.VMEM((len(DIRS), EXT, 256), F32),
             pltpu.VMEM((EXT, 256), F32),
             pltpu.VMEM((ROWS, WIDE), BF16),
-            pltpu.VMEM((G * G, ROW_BLK, 128), BF16),
-            pltpu.VMEM((OWNERS, 2, ROW_BLK, 128), BF16),
+            pltpu.VMEM((G * G, *block), BF16),
+            pltpu.VMEM((OWNERS, *block), BF16),
+            pltpu.VMEM((N, SECOND, *block), BF16),
+            pltpu.VMEM((N, SECOND, *block), BF16),
+            pltpu.VMEM((N, N, *block), BF16),
+            pltpu.VMEM((2, 128), jnp.int32),
+            pltpu.SMEM((2, 128), jnp.int32),
+            pltpu.VMEM((N, 2, N, 128), jnp.int32),
+            pltpu.VMEM((N, 2, N, 128), jnp.int32),
             pltpu.VMEM((N, N, 128), jnp.int32),
             pltpu.VMEM((N, N, 128), jnp.int32),
-            pltpu.SemaphoreType.DMA((NCHUNK,)),
-            pltpu.SemaphoreType.DMA((2,)),
-        ] + [pltpu.SemaphoreType.DMA] * 8,
+            pltpu.VMEM((N, 128), jnp.int32),
+            pltpu.VMEM((N, N, 128), jnp.int32),
+            pltpu.VMEM((8, 128), F32),
+            pltpu.VMEM((N, 128), jnp.int32),
+            dma((NCHUNK + 4,)),
+            dma((5,)),
+        ] + [dma] * 14,
         compiler_params=pltpu.CompilerParams(
-            collective_id=1, has_side_effects=True, vmem_limit_bytes=40 << 20
+            collective_id=1, has_side_effects=True, vmem_limit_bytes=61 << 20
         ),
         cost_estimate=pl.CostEstimate(
             flops=4 * ROWS * ROWS * EXT3, bytes_accessed=6 << 20, transcendentals=2 * EXT3
         ),
-    )(sel, basis.reshape(ROWS, EXT3), density_blocks, pair_groups, meta)
-
-    ks_blocks = pl.pallas_call(
-        store_kernel,
-        name="store_blocks",
-        out_shape=jax.ShapeDtypeStruct((PAIRS, 4096), BF16),
-        in_specs=[smem, vmem],
-        out_specs=vmem,
-        scratch_shapes=[pltpu.VMEM(((PAIRS + 1) * ROW_BLK, 128), F32)],
-        compiler_params=pltpu.CompilerParams(vmem_limit_bytes=32 << 20),
-    )(mx.reshape(N * N, 128), recv)
-    potential = pot.reshape(8, 8, EXT)[:, :, RIM:RIM + 8]
-    return ks_blocks, potential
+    )(
+        basis.reshape(ROWS, EXT3), density_blocks, pair_groups,
+        owner.reshape(1, PAIRS), owner_slot.reshape(1, PAIRS),
+    )
+    recv2 = recv2.reshape(OWNERS, *block)
+    return lax.cond(
+        flag[0, 0] > 0,
+        lambda: resend(pair_groups, owner, owner_slot, table, slots, recv, recv2, pot),
+        lambda: store(slots, recv, recv2, pot),
+    )
 
 
 def solution(mesh):

time: 63.7 us -> 53.4 us (0.84)
  local copies, waits for them, and re-layouts: 4.86 us -> 0.01 us
  Pallas kernels: 55.3 us -> 51.9 us
  other arithmetic: 2.54 us -> 0 us
  between operations: 0.66 us -> 1.32 us
    unnamed x6, local copies, waits for them, and re-layouts: 3.72 us -> 0.01 us
    pallas_call x1, Pallas kernels: 51.7 us -> 48.4 us  [per_device(): pl.pallas_call(main_kernel, name='collocate_exchange', out_shape=(jax.Sha...]
    reduce_sum x2 -> x0, other arithmetic: 1.01 us -> none  [the longest x1 0.91 us: per_device(): rank = jnp.sum(earlier.astype(jnp.int32), axis=1)]
    slice x2 -> x0, local copies, waits for them, and re-layouts: 0.77 us -> none  [the longest x1 0.7 us: per_device(): potential = pot.reshape(8, 8, EXT)[:, :, RIM:RIM + 8]]
    broadcast_in_dim x1 -> x0, other arithmetic: 0.77 us -> none  [per_device(): sel = jnp.sum(jnp.where(match, codes[None, :], 0), axis=1)]
    add x1 -> x0, other arithmetic: 0.67 us -> none  [per_device(): place = rank * OWNERS + names]
where the time goes in v2:
time: 53.4 us; the launch traced here: 53.2 us
  Pallas kernels  51.9 us (97%)
  between operations  1.32 us (2%)
    pallas_call x1, Pallas kernels, per_device(): pl.pallas_call(main_kernel, name='collocate_exchange', out_shape=(jax.Sha...  48.4 us
    pallas_call x1, Pallas kernels, store(): pl.pallas_call(store_kernel, name='store_blocks', out_shape=(jax.ShapeDty...  3.49 us

profile of v2, /device:TPU:1, one launch (start us, length us, event | category | flops | bytes accessed | tf_op | source)
XLA Modules:
  0.0 53.2 jit_solution(7617726566149466406)
XLA Ops:
  0.6 0.0 copy-start.1
  0.6 0.0 copy-start.2
  0.7 0.0 copy-start.3
  0.7 48.4 %collocate_exchange.1 = (bf16[64,32,128]{2,1,0:T(8,128)(2,1)S(1)}, bf16[8,8,32,128]{3,2,1,0:T(8,128)(2,1)S(1)}, s32[8,128]{1,0:T(8,128)S(1)}, s32[1,1]{1,0:T(1,1...) custom-call(bf16[448,4096]{1,0:T(8,128)(2,1)} %bitcast.19, bf16[48,4096]{1,0:T(8,128)(2,1)} %blocks_ref.1, ...), custom_call_target="tpu_custom_call" | custom-call | flops 3288334336 | bytes 6291456 | tf_op jit(solution)/shard_map/collocate_exchange/pallas_call | solution.py:483
  49.7 0.0 copy-done.1
  49.7 0.0 copy-done.2
  49.7 0.0 copy-done.3
  49.7 3.5 %conditional.1 = ((bf16[48,4096]{1,0:T(8,128)(2,1)}, f32[8,8,8]{2,1,0:T(8,128)})) conditional(s32[]{:T(128)} %bitcast.8, (bf16[8,8,32,128]{3,2,1,0:T(8,128)(2,1)S(1)}, s32[8,128]{1,0:T(8,128)S(1)}, bf16[64,32,128]{2,1,0:T(8,128)(2,1)S(1)}, f32[8,128]{1,0:T(8,128)S(1)}) %tuple.13, (s32[8,128]{1,0:T(8,128)S(1)}, s32[48,1]{0,1:T(1,128)S(1)}, ...), branch_computations={%region_0.0_spmd, %region_1.5_spmd} | conditional | flops 25724304 | bytes 5722124 | solution.py:539
  49.7 3.5 %store_blocks.2 = (bf16[48,4096]{1,0:T(8,128)(2,1)}, f32[8,8,8]{2,1,0:T(8,128)}) custom-call(s32[8,128]{1,0:T(8,128)S(1)} %get-tuple-element.23.slots_ref, bf16[64,32,128]{2,1,0:T(8,128)(2,1)S(1)} %get-tuple-element.24.recv_ref, bf16[64,32,128]{2,1,0:T(8,128)(2,1)S(1)} %bitcast.14, f32[8,128]{1,0:T(8,128)S(1)} %get-tuple-element.26.pot_ref), custom_call_target="tpu_custom_call" | custom-call | tf_op jit(solution)/shard_map/cond/branch_0_fun/store_blocks/pallas_call | solution.py:435
Async XLA Ops:
  0.6 49.1 %copy-start.1 = (s32[48,1]{0,1:T(1,128)S(1)}, s32[48,1]{0,1:T(1,128)}, u32[]{:S(2)}) copy-start(s32[48,1]{0,1:T(1,128)} %param.10) | copy-start | bytes 580
  0.6 49.1 %copy-start.2 = (s32[2,48]{1,0:T(2,128)S(1)}, s32[2,48]{1,0:T(2,128)}, u32[]{:S(2)}) copy-start(s32[2,48]{1,0:T(2,128)} %groups_ref.1) | copy-start | bytes 1156
  0.7 49.1 %copy-start.3 = (s32[48]{0:T(128)S(1)}, s32[48]{0:T(128)}, u32[]{:S(2)}) copy-start(s32[48]{0:T(128)} %param.11) | copy-start | bytes 580

commit v3 on v2

--- a/solution.py
+++ b/solution.py
@@ -25,7 +25,7 @@
 F32 = jnp.float32
 BF16 = jnp.bfloat16
 
-CHUNK = 512
+CHUNK = 2048
 NCHUNK = EXT3 // CHUNK
 
 DIRS = [(a, b, c) for c in (0, 1, -1) for a in (0, 1, -1) for b in (0, 1, -1) if (a, b, c) != (0, 0, 0)]
@@ -35,7 +35,6 @@
 PEERS = OWNERS - 1 + len(OUT_PLANE) + len(FAR_Z)
 FAR_FIRST = (4, 3, 5, 2, 6, 1, 7, 0)
 SECOND = 3
-PARTS = 4
 FLAG = 128
 
 
@@ -97,7 +96,55 @@
     split_rows = jnp.where(c64 == 2 * (r64 % 32) + r64 // 32, 1.0, 0.0).astype(BF16)
     join_rows = jnp.where(r64 == 2 * (c64 % 32) + c64 // 32, 1.0, 0.0).astype(BF16)
 
-    for copy in small[:3]:
+    small[0].wait()
+    codes = gv[0:1, :] * G + gv[1:2, :]
+    pick = jnp.where(
+        lax.broadcasted_iota(jnp.int32, (CODES, PAIRS), 0) == codes, 1.0, 0.0
+    ).astype(BF16)
+    small[3].wait()
+    for n in range(8):
+        part = jnp.dot(pick, blk[:, n * 512:(n + 1) * 512], preferred_element_type=F32)
+        for q in range(4):
+            a3[pl.ds(n * 4 + q, CODES, stride=ROW_BLK), :] = part[:, q * 128:(q + 1) * 128]
+    for a in range(G):
+        for bp in range(4):
+            even = a3[(a * G + 2 * bp) * ROW_BLK:(a * G + 2 * bp + 1) * ROW_BLK, :]
+            if 2 * bp + 1 < G:
+                odd = a3[(a * G + 2 * bp + 1) * ROW_BLK:(a * G + 2 * bp + 2) * ROW_BLK, :]
+            else:
+                odd = jnp.zeros((ROW_BLK, 128), F32)
+            top = jnp.where(low, even, pltpu.roll(odd, 64, axis=1))
+            bottom = jnp.where(low, pltpu.roll(even, 64, axis=1), odd)
+            mperm[a * 64:a * 64 + 32, bp * 128:(bp + 1) * 128] = top.astype(BF16)
+            mperm[a * 64 + 32:(a + 1) * 64, bp * 128:(bp + 1) * 128] = bottom.astype(BF16)
+        mat[a * 64:(a + 1) * 64, :] = jnp.dot(
+            join_rows, mperm[a * 64:(a + 1) * 64, :], preferred_element_type=F32
+        ).astype(BF16)
+
+    for n in range(NCHUNK):
+        loads[n].wait()
+        cols = slice(n * CHUNK, (n + 1) * CHUNK)
+        part = phi[:, cols]
+        image = jnp.dot(mat[:, :ROWS], part, preferred_element_type=F32)
+        line = jnp.sum(part.astype(F32) * image, axis=0, keepdims=True)
+        for q in range(CHUNK // 256):
+            x = n * (CHUNK // 256) + q
+            rho[x:x + 1, :] = line[:, q * 256:(q + 1) * 256]
+
+    pl.semaphore_wait(barrier, PEERS)
+
+    for n, (a, b, c) in enumerate(DIRS):
+        src = rho.at[half(a, pl.ds(0, 8), pl.ds(8, 8), pl.ds(0, 16)),
+                     half(b, pl.ds(0, 128), pl.ds(128, 128), pl.ds(0, 256))]
+        dst = hr.at[n, half(-a, pl.ds(0, 8), pl.ds(8, 8), pl.ds(0, 16)),
+                    half(-b, pl.ds(0, 128), pl.ds(128, 128), pl.ds(0, 256))]
+        pltpu.make_async_remote_copy(
+            src_ref=src, dst_ref=dst, send_sem=halo_send, recv_sem=halo_recv,
+            device_id=(lax.rem(i + a + N, N), lax.rem(j + b + N, N), lax.rem(k + c + N, N)),
+            device_id_type=MESH,
+        ).start()
+
+    for copy in small[1:3]:
         copy.wait()
     row = lax.broadcasted_iota(jnp.int32, (PAIRS, PAIRS), 0)
     col = lax.broadcasted_iota(jnp.int32, (PAIRS, PAIRS), 1)
@@ -108,7 +155,6 @@
     def count(mask, axis):
         return jnp.sum(jnp.where(mask, 1, 0), axis=axis, keepdims=True)
 
-    codes = gv[0:1, :] * G + gv[1:2, :]
     own_r = ov[...]
     own_c = upright(own_r)
     code_c = upright(codes)
@@ -144,52 +190,6 @@
         meta[t, 0] = tile[t * N:(t + 1) * N]
         meta[t, 1] = index[t * N:(t + 1) * N]
 
-    pick = jnp.where(
-        lax.broadcasted_iota(jnp.int32, (CODES, PAIRS), 0) == codes, 1.0, 0.0
-    ).astype(BF16)
-    small[3].wait()
-    for n in range(8):
-        part = jnp.dot(pick, blk[:, n * 512:(n + 1) * 512], preferred_element_type=F32)
-        for q in range(4):
-            a3[pl.ds(n * 4 + q, CODES, stride=ROW_BLK), :] = part[:, q * 128:(q + 1) * 128]
-    for a in range(G):
-        for bp in range(4):
-            even = a3[(a * G + 2 * bp) * ROW_BLK:(a * G + 2 * bp + 1) * ROW_BLK, :]
-            if 2 * bp + 1 < G:
-                odd = a3[(a * G + 2 * bp + 1) * ROW_BLK:(a * G + 2 * bp + 2) * ROW_BLK, :]
-            else:
-                odd = jnp.zeros((ROW_BLK, 128), F32)
-            top = jnp.where(low, even, pltpu.roll(odd, 64, axis=1))
-            bottom = jnp.where(low, pltpu.roll(even, 64, axis=1), odd)
-            mperm[a * 64:a * 64 + 32, bp * 128:(bp + 1) * 128] = top.astype(BF16)
-            mperm[a * 64 + 32:(a + 1) * 64, bp * 128:(bp + 1) * 128] = bottom.astype(BF16)
-        mat[a * 64:(a + 1) * 64, :] = jnp.dot(
-            join_rows, mperm[a * 64:(a + 1) * 64, :], preferred_element_type=F32
-        ).astype(BF16)
-
-    for n in range(NCHUNK):
-        loads[n].wait()
-        cols = slice(n * CHUNK, (n + 1) * CHUNK)
-        part = phi[:, cols]
-        image = jnp.dot(mat[:, :ROWS], part, preferred_element_type=F32)
-        line = jnp.sum(part.astype(F32) * image, axis=0, keepdims=True)
-        for q in range(CHUNK // 256):
-            x = n * (CHUNK // 256) + q
-            rho[x:x + 1, :] = line[:, q * 256:(q + 1) * 256]
-
-    pl.semaphore_wait(barrier, PEERS)
-
-    for n, (a, b, c) in enumerate(DIRS):
-        src = rho.at[half(a, pl.ds(0, 8), pl.ds(8, 8), pl.ds(0, 16)),
-                     half(b, pl.ds(0, 128), pl.ds(128, 128), pl.ds(0, 256))]
-        dst = hr.at[n, half(-a, pl.ds(0, 8), pl.ds(8, 8), pl.ds(0, 16)),
-                    half(-b, pl.ds(0, 128), pl.ds(128, 128), pl.ds(0, 256))]
-        pltpu.make_async_remote_copy(
-            src_ref=src, dst_ref=dst, send_sem=halo_send, recv_sem=halo_recv,
-            device_id=(lax.rem(i + a + N, N), lax.rem(j + b + N, N), lax.rem(k + c + N, N)),
-            device_id_type=MESH,
-        ).start()
-
     def send_z(t, carry):
         ti = lax.rem(i + t, N)
         pltpu.make_async_remote_copy(
@@ -236,21 +236,6 @@
     pot_copy = pltpu.make_async_copy(potv, pot_ref, own_sem.at[3])
     pot_copy.start()
 
-    bytes_wait(mz.at[0:N - 1], mz_recv)
-    for t in range(N):
-        xs[t] = mz[:, 0, t, :]
-
-    def send_x(t, carry):
-        tj = lax.rem(j + t, N)
-        pltpu.make_async_remote_copy(
-            src_ref=xs.at[tj], dst_ref=mx.at[j], send_sem=mx_send, recv_sem=mx_recv,
-            device_id=(i, tj, k), device_id_type=MESH,
-        ).start()
-        return carry
-
-    lax.fori_loop(1, N, send_x, 0)
-    mx[j] = xs[j]
-
     for x in range(EXT):
         cols = slice(x * 256, (x + 1) * 256)
         wgt[:, cols] = (phi[:, cols].astype(F32) * vpot[x:x + 1, :]).astype(BF16)
@@ -270,6 +255,21 @@
                     low, pltpu.roll(top, 64, axis=1), bottom
                 ).astype(BF16)
 
+    bytes_wait(mz.at[0:N - 1], mz_recv)
+    for t in range(N):
+        xs[t] = mz[:, 0, t, :]
+
+    def send_x(t, carry):
+        tj = lax.rem(j + t, N)
+        pltpu.make_async_remote_copy(
+            src_ref=xs.at[tj], dst_ref=mx.at[j], send_sem=mx_send, recv_sem=mx_recv,
+            device_id=(i, tj, k), device_id_type=MESH,
+        ).start()
+        return carry
+
+    lax.fori_loop(1, N, send_x, 0)
+    mx[j] = xs[j]
+
     sel_copy.wait()
     keep = pltpu.make_async_copy(table, table_ref, own_sem.at[0])
     keep.start()
@@ -382,56 +382,28 @@
     bytes_wait(recv_ref.at[0:OWNERS - 1], blk_recv)
 
 
-def store_kernel(
-    slots_ref, recv_ref, recv2_ref, pot_ref, out_ref, pot_out,
-    acc, slots, got, got2, pot, cells, rows, sem, out_sem,
-):
-    def start(src, dst, at):
-        copy = pltpu.make_async_copy(src, dst, at)
-        copy.start()
-        return copy
-
-    few = OWNERS // PARTS
-    slots_in = start(slots_ref, slots, sem.at[2 * PARTS])
-    pot_in = start(pot_ref, pot, sem.at[2 * PARTS + 1])
-    parts = []
-    for n in range(PARTS):
-        part = pl.ds(n * few, few)
-        parts.append((
-            start(recv_ref.at[part], got.at[part], sem.at[2 * n]),
-            start(recv2_ref.at[part], got2.at[part], sem.at[2 * n + 1]),
-        ))
+def store_kernel(slots_ref, recv_ref, recv2_ref, pot_ref, out_ref, pot_out, acc):
     acc[...] = jnp.zeros_like(acc)
-    pot_in.wait()
+    pot = pot_ref[...]
     for y in range(8):
-        cells[:, y, :] = pot[:, y * EXT + RIM:y * EXT + RIM + 8]
-    outs = [start(cells, pot_out, out_sem.at[PARTS])]
+        pot_out[:, y, :] = pot[:, y * EXT + RIM:y * EXT + RIM + 8]
 
     def add(t, carry):
-        for rank, ref in enumerate((got, got2)):
-            slot = slots[0, rank * OWNERS + t]
+        for rank, ref in enumerate((recv_ref, recv2_ref)):
+            slot = slots_ref[0, rank * OWNERS + t]
             slot = jnp.where(slot < 0, PAIRS, slot)
             at = pl.ds(pl.multiple_of(slot * ROW_BLK, ROW_BLK), ROW_BLK)
             acc[at, :] += ref[t].astype(F32)
         return carry
 
-    slots_in.wait()
-    for n in range(PARTS):
-        for copy in parts[n]:
-            copy.wait()
-        lax.fori_loop(n * few, (n + 1) * few, add, 0, unroll=4)
-    wide = ROW_BLK // PARTS
-    for n in range(PARTS):
-        for c in range(n * wide, (n + 1) * wide):
-            rows[:, c * 128:(c + 1) * 128] = acc[pl.ds(c, PAIRS, stride=ROW_BLK), :].astype(BF16)
-        cols = pl.ds(n * wide * 128, wide * 128)
-        outs.append(start(rows.at[:, cols], out_ref.at[:, cols], out_sem.at[n]))
-    for copy in outs:
-        copy.wait()
+    lax.fori_loop(0, OWNERS, add, 0, unroll=4)
+    for c in range(ROW_BLK):
+        out_ref[:, c * 128:(c + 1) * 128] = acc[pl.ds(c, PAIRS, stride=ROW_BLK), :].astype(BF16)
 
 
 def store(slots, recv, recv2, pot):
-    hbm = pl.BlockSpec(memory_space=pl.ANY)
+    vmem = pl.BlockSpec(memory_space=pltpu.VMEM)
+    smem = pl.BlockSpec(memory_space=pltpu.SMEM)
     return pl.pallas_call(
         store_kernel,
         name="store_blocks",
@@ -439,20 +411,10 @@
             jax.ShapeDtypeStruct((PAIRS, 4096), BF16),
             jax.ShapeDtypeStruct((8, 8, 8), F32),
         ),
-        in_specs=[hbm] * 4,
-        out_specs=(hbm, hbm),
-        scratch_shapes=[
-            pltpu.VMEM(((PAIRS + 1) * ROW_BLK, 128), F32),
-            pltpu.SMEM((8, 128), jnp.int32),
-            pltpu.VMEM((OWNERS, ROW_BLK, 128), BF16),
-            pltpu.VMEM((OWNERS, ROW_BLK, 128), BF16),
-            pltpu.VMEM((8, 128), F32),
-            pltpu.VMEM((8, 8, 8), F32),
-            pltpu.VMEM((PAIRS, 4096), BF16),
-            pltpu.SemaphoreType.DMA((2 * PARTS + 2,)),
-            pltpu.SemaphoreType.DMA((PARTS + 1,)),
-        ],
-        compiler_params=pltpu.CompilerParams(vmem_limit_bytes=61 << 20),
+        in_specs=[smem, vmem, vmem, vmem],
+        out_specs=(vmem, vmem),
+        scratch_shapes=[pltpu.VMEM(((PAIRS + 1) * ROW_BLK, 128), F32)],
+        compiler_params=pltpu.CompilerParams(vmem_limit_bytes=16 << 20),
     )(slots, recv, recv2, pot)
 
 

time: 53.4 us -> 51.4 us (0.963)
  the two profiles are of different devices: /device:TPU:1 before, /device:TPU:9 now
where the time goes in v3:
time: 51.4 us; the launch traced here: 51.2 us
  Pallas kernels  50 us (97%)
  between operations  1.25 us (2%)
    pallas_call x1, Pallas kernels, per_device(): pl.pallas_call(main_kernel, name='collocate_exchange', out_shape=(jax.Sha...  47.3 us
    pallas_call x1, Pallas kernels, store(): pl.pallas_call(store_kernel, name='store_blocks', out_shape=(jax.ShapeDty...  2.64 us

profile of v3, /device:TPU:9, one launch (start us, length us, event | category | flops | bytes accessed | tf_op | source)
XLA Modules:
  0.0 51.2 jit_solution(5618327176121951064)
XLA Ops:
  0.6 0.0 copy-start
  0.6 0.0 copy-start.1
  0.7 0.0 copy-start.2
  0.7 47.3 %collocate_exchange.1 = (bf16[64,32,128]{2,1,0:T(8,128)(2,1)S(1)}, bf16[8,8,32,128]{3,2,1,0:T(8,128)(2,1)S(1)}, s32[8,128]{1,0:T(8,128)S(1)}, s32[1,1]{1,0:T(1,1...) custom-call(bf16[448,4096]{1,0:T(8,128)(2,1)} %bitcast.19, bf16[48,4096]{1,0:T(8,128)(2,1)} %blocks_ref.1, ...), custom_call_target="tpu_custom_call" | custom-call | flops 3288334336 | bytes 6291456 | tf_op jit(solution)/shard_map/collocate_exchange/pallas_call | solution.py:445
  48.6 0.0 copy-done
  48.6 0.0 copy-done.1
  48.6 0.0 copy-done.2
  48.6 2.6 %conditional.1 = ((bf16[48,4096]{1,0:T(8,128)(2,1)}, f32[8,8,8]{2,1,0:T(8,128)})) conditional(s32[]{:T(128)} %bitcast.8, (bf16[8,8,32,128]{3,2,1,0:T(8,128)(2,1)S(1)}, s32[8,128]{1,0:T(8,128)S(1)}, bf16[64,32,128]{2,1,0:T(8,128)(2,1)S(1)}, f32[8,128]{1,0:T(8,128)S(1)}) %tuple.13, (s32[8,128]{1,0:T(8,128)S(1)}, s32[48,1]{0,1:T(1,128)S(1)}, ...), branch_computations={%region_0.0_spmd, %region_1.5_spmd} | conditional | flops 25724304 | bytes 3624944 | solution.py:501
  48.6 2.6 %store_blocks.2 = (bf16[48,4096]{1,0:T(8,128)(2,1)}, f32[8,8,8]{2,1,0:T(8,128)}) custom-call(s32[8,128]{1,0:T(8,128)S(1)} %get-tuple-element.23.slots_ref, bf16[64,32,128]{2,1,0:T(8,128)(2,1)S(1)} %get-tuple-element.24.recv_ref, bf16[64,32,128]{2,1,0:T(8,128)(2,1)S(1)} %bitcast.14, f32[8,128]{1,0:T(8,128)S(1)} %get-tuple-element.26.pot_ref), custom_call_target="tpu_custom_call" | custom-call | tf_op jit(solution)/shard_map/cond/branch_0_fun/store_blocks/pallas_call | solution.py:407
Async XLA Ops:
  0.6 47.9 %copy-start = (s32[48,1]{0,1:T(1,128)S(1)}, s32[48,1]{0,1:T(1,128)}, u32[]{:S(2)}) copy-start(s32[48,1]{0,1:T(1,128)} %param.10) | copy-start | bytes 580
  0.6 47.9 %copy-start.1 = (s32[2,48]{1,0:T(2,128)S(1)}, s32[2,48]{1,0:T(2,128)}, u32[]{:S(2)}) copy-start(s32[2,48]{1,0:T(2,128)} %groups_ref.1) | copy-start | bytes 1156
  0.7 47.9 %copy-start.2 = (s32[48]{0:T(128)S(1)}, s32[48]{0:T(128)}, u32[]{:S(2)}) copy-start(s32[48]{0:T(128)} %param.11) | copy-start | bytes 580

commit v4 on v3

--- a/solution.py
+++ b/solution.py
@@ -72,21 +72,14 @@
         loads.append(copy)
 
     barrier = pltpu.get_barrier_semaphore()
-
-    def greet(t, carry):
+    gxs = [lax.rem(i + t, N) for t in range(N)]
+    gys = [lax.rem(j + t, N) for t in range(N)]
+    gzs = [lax.rem(k + t, N) for t in range(N)]
+    peers = [(a % N, b % N, c % N) for a, b, c in OUT_PLANE + [(0, 0, t) for t in FAR_Z]]
+    peers += [(a, b, 0) for a in FAR_FIRST for b in (4, 3, 5, 2, 6, 1, 7, 0) if (a, b) != (0, 0)]
+    for a, b, c in peers:
         pl.semaphore_signal(
-            barrier, inc=1,
-            device_id=(lax.rem(i + t // N, N), lax.rem(j + lax.rem(t, N), N), k),
-            device_id_type=MESH,
-        )
-        return carry
-
-    lax.fori_loop(1, OWNERS, greet, 0)
-    for a, b, c in OUT_PLANE + [(0, 0, t) for t in FAR_Z]:
-        pl.semaphore_signal(
-            barrier, inc=1,
-            device_id=(lax.rem(i + a + N, N), lax.rem(j + b + N, N), lax.rem(k + c + N, N)),
-            device_id_type=MESH,
+            barrier, inc=1, device_id=(gxs[a], gys[b], gzs[c]), device_id_type=MESH
         )
 
     lane = lax.broadcasted_iota(jnp.int32, (ROW_BLK, 128), 1)

time: 51.4 us -> 48.9 us (0.951)
  the two profiles are of different devices: /device:TPU:9 before, /device:TPU:1 now
where the time goes in v4:
time: 48.9 us; the launch traced here: 48.8 us
  Pallas kernels  47.5 us (97%)
  between operations  1.25 us (3%)
    pallas_call x1, Pallas kernels, per_device(): pl.pallas_call(main_kernel, name='collocate_exchange', out_shape=(jax.Sha...  44.9 us
    pallas_call x1, Pallas kernels, store(): pl.pallas_call(store_kernel, name='store_blocks', out_shape=(jax.ShapeDty...  2.65 us

profile of v4, /device:TPU:1, one launch (start us, length us, event | category | flops | bytes accessed | tf_op | source)
XLA Modules:
  0.0 48.8 jit_solution(17096357682712766645)
XLA Ops:
  0.6 0.0 copy-start
  0.6 0.0 copy-start.1
  0.7 0.0 copy-start.2
  0.7 44.9 %collocate_exchange.1 = (bf16[64,32,128]{2,1,0:T(8,128)(2,1)S(1)}, bf16[8,8,32,128]{3,2,1,0:T(8,128)(2,1)S(1)}, s32[8,128]{1,0:T(8,128)S(1)}, s32[1,1]{1,0:T(1,1...) custom-call(bf16[448,4096]{1,0:T(8,128)(2,1)} %bitcast.19, bf16[48,4096]{1,0:T(8,128)(2,1)} %blocks_ref.1, ...), custom_call_target="tpu_custom_call" | custom-call | flops 3288334336 | bytes 6291456 | tf_op jit(solution)/shard_map/collocate_exchange/pallas_call | solution.py:438
  46.1 0.0 copy-done
  46.1 0.0 copy-done.1
  46.1 0.0 copy-done.2
  46.1 2.7 %conditional.1 = ((bf16[48,4096]{1,0:T(8,128)(2,1)}, f32[8,8,8]{2,1,0:T(8,128)})) conditional(s32[]{:T(128)} %bitcast.8, (bf16[8,8,32,128]{3,2,1,0:T(8,128)(2,1)S(1)}, s32[8,128]{1,0:T(8,128)S(1)}, bf16[64,32,128]{2,1,0:T(8,128)(2,1)S(1)}, f32[8,128]{1,0:T(8,128)S(1)}) %tuple.13, (s32[8,128]{1,0:T(8,128)S(1)}, s32[48,1]{0,1:T(1,128)S(1)}, ...), branch_computations={%region_0.0_spmd, %region_1.5_spmd} | conditional | flops 25724304 | bytes 3624944 | solution.py:494
  46.1 2.7 %store_blocks.2 = (bf16[48,4096]{1,0:T(8,128)(2,1)}, f32[8,8,8]{2,1,0:T(8,128)}) custom-call(s32[8,128]{1,0:T(8,128)S(1)} %get-tuple-element.23.slots_ref, bf16[64,32,128]{2,1,0:T(8,128)(2,1)S(1)} %get-tuple-element.24.recv_ref, bf16[64,32,128]{2,1,0:T(8,128)(2,1)S(1)} %bitcast.14, f32[8,128]{1,0:T(8,128)S(1)} %get-tuple-element.26.pot_ref), custom_call_target="tpu_custom_call" | custom-call | tf_op jit(solution)/shard_map/cond/branch_0_fun/store_blocks/pallas_call | solution.py:400
Async XLA Ops:
  0.6 45.5 %copy-start = (s32[48,1]{0,1:T(1,128)S(1)}, s32[48,1]{0,1:T(1,128)}, u32[]{:S(2)}) copy-start(s32[48,1]{0,1:T(1,128)} %param.10) | copy-start | bytes 580
  0.6 45.5 %copy-start.1 = (s32[2,48]{1,0:T(2,128)S(1)}, s32[2,48]{1,0:T(2,128)}, u32[]{:S(2)}) copy-start(s32[2,48]{1,0:T(2,128)} %groups_ref.1) | copy-start | bytes 1156
  0.7 45.5 %copy-start.2 = (s32[48]{0:T(128)S(1)}, s32[48]{0:T(128)}, u32[]{:S(2)}) copy-start(s32[48]{0:T(128)} %param.11) | copy-start | bytes 580

commit v5 on v4

--- a/solution.py
+++ b/solution.py
@@ -248,6 +248,24 @@
                     low, pltpu.roll(top, 64, axis=1), bottom
                 ).astype(BF16)
 
+    sel_copy.wait()
+    keep = pltpu.make_async_copy(table, table_ref, own_sem.at[0])
+    keep.start()
+
+    def pack_second(ti):
+        for c in range(SECOND):
+            z2s[ti, c] = table[sels[1, ti * SECOND + c]]
+
+    for di in FAR_FIRST[:-1]:
+        ti = lax.rem(i + di, N)
+        pack_second(ti)
+        pltpu.make_async_remote_copy(
+            src_ref=z2s.at[ti], dst_ref=z2r.at[i], send_sem=z2_send, recv_sem=z2_recv,
+            device_id=(ti, j, k), device_id_type=MESH,
+        ).start()
+    pack_second(i)
+    z2r[i] = z2s[i]
+
     bytes_wait(mz.at[0:N - 1], mz_recv)
     for t in range(N):
         xs[t] = mz[:, 0, t, :]
@@ -262,28 +280,6 @@
 
     lax.fori_loop(1, N, send_x, 0)
     mx[j] = xs[j]
-
-    sel_copy.wait()
-    keep = pltpu.make_async_copy(table, table_ref, own_sem.at[0])
-    keep.start()
-
-    def pack_second(t, carry):
-        for c in range(SECOND):
-            z2s[t, c] = table[sels[1, t * SECOND + c]]
-        return carry
-
-    lax.fori_loop(0, N, pack_second, 0)
-
-    def send_second(t, carry):
-        ti = lax.rem(i + t, N)
-        pltpu.make_async_remote_copy(
-            src_ref=z2s.at[ti], dst_ref=z2r.at[i], send_sem=z2_send, recv_sem=z2_recv,
-            device_id=(ti, j, k), device_id_type=MESH,
-        ).start()
-        return carry
-
-    lax.fori_loop(1, N, send_second, 0)
-    z2r[i] = z2s[i]
 
     for di in FAR_FIRST:
         ti = lax.rem(i + di, N)
@@ -332,26 +328,23 @@
     fr[k] = over
 
     bytes_wait(z2r.at[0:N - 1], z2_recv)
-    for t in range(N):
-        def place_second(a, carry, t=t):
-            index = jnp.broadcast_to(mz[a, 1, t:t + 1, :], (ROW_BLK, 128))
+    for dj in FAR_FIRST:
+        tj = lax.rem(j + dj, N)
+
+        def place_second(a, carry, tj=tj):
+            index = jnp.broadcast_to(mz[a, 1, pl.ds(tj, 1), :], (ROW_BLK, 128))
             total = jnp.zeros((ROW_BLK, 128), F32)
             for c in range(SECOND):
                 total = jnp.where(index == c, z2r[a, c].astype(F32), total)
-            x2s[t, a] = total.astype(BF16)
+            x2s[tj, a] = total.astype(BF16)
             return carry
 
         lax.fori_loop(0, N, place_second, 0)
-
-    def forward(t, carry):
-        tj = lax.rem(j + t, N)
-        pltpu.make_async_remote_copy(
-            src_ref=x2s.at[tj], dst_ref=recv2_ref.at[j], send_sem=x2_send, recv_sem=x2_recv,
-            device_id=(i, tj, k), device_id_type=MESH,
-        ).start()
-        return carry
-
-    lax.fori_loop(1, N, forward, 0)
+        if dj:
+            pltpu.make_async_remote_copy(
+                src_ref=x2s.at[tj], dst_ref=recv2_ref.at[j], send_sem=x2_send, recv_sem=x2_recv,
+                device_id=(i, tj, k), device_id_type=MESH,
+            ).start()
     own2 = pltpu.make_async_copy(x2s.at[j], recv2_ref.at[j], own_sem.at[2])
     own2.start()
 

time: 48.9 us -> 47.5 us (0.971)
  Pallas kernels: 47.5 us -> 46.2 us
    pallas_call x1, Pallas kernels: 44.9 us -> 43.5 us  [per_device(): pl.pallas_call(main_kernel, name='collocate_exchange', out_shape=(jax.Sha...]
where the time goes in v5:
time: 47.5 us; the launch traced here: 47.4 us
  Pallas kernels  46.2 us (97%)
  between operations  1.25 us (3%)
    pallas_call x1, Pallas kernels, per_device(): pl.pallas_call(main_kernel, name='collocate_exchange', out_shape=(jax.Sha...  43.5 us
    pallas_call x1, Pallas kernels, store(): pl.pallas_call(store_kernel, name='store_blocks', out_shape=(jax.ShapeDty...  2.67 us

profile of v5, /device:TPU:1, one launch (start us, length us, event | category | flops | bytes accessed | tf_op | source)
XLA Modules:
  0.0 47.4 jit_solution(17734772722296757204)
XLA Ops:
  0.6 0.0 copy-start
  0.6 0.0 copy-start.1
  0.7 0.0 copy-start.2
  0.7 43.5 %collocate_exchange.1 = (bf16[64,32,128]{2,1,0:T(8,128)(2,1)S(1)}, bf16[8,8,32,128]{3,2,1,0:T(8,128)(2,1)S(1)}, s32[8,128]{1,0:T(8,128)S(1)}, s32[1,1]{1,0:T(1,1...) custom-call(bf16[448,4096]{1,0:T(8,128)(2,1)} %bitcast.19, bf16[48,4096]{1,0:T(8,128)(2,1)} %blocks_ref.1, ...), custom_call_target="tpu_custom_call" | custom-call | flops 3288334336 | bytes 6291456 | tf_op jit(solution)/shard_map/collocate_exchange/pallas_call | solution.py:431
  44.7 0.0 copy-done
  44.7 0.0 copy-done.1
  44.7 0.0 copy-done.2
  44.8 2.7 %conditional.1 = ((bf16[48,4096]{1,0:T(8,128)(2,1)}, f32[8,8,8]{2,1,0:T(8,128)})) conditional(s32[]{:T(128)} %bitcast.8, (bf16[8,8,32,128]{3,2,1,0:T(8,128)(2,1)S(1)}, s32[8,128]{1,0:T(8,128)S(1)}, bf16[64,32,128]{2,1,0:T(8,128)(2,1)S(1)}, f32[8,128]{1,0:T(8,128)S(1)}) %tuple.13, (s32[8,128]{1,0:T(8,128)S(1)}, s32[48,1]{0,1:T(1,128)S(1)}, ...), branch_computations={%region_0.0_spmd, %region_1.5_spmd} | conditional | flops 25724304 | bytes 3624944 | solution.py:487
  44.8 2.7 %store_blocks.2 = (bf16[48,4096]{1,0:T(8,128)(2,1)}, f32[8,8,8]{2,1,0:T(8,128)}) custom-call(s32[8,128]{1,0:T(8,128)S(1)} %get-tuple-element.23.slots_ref, bf16[64,32,128]{2,1,0:T(8,128)(2,1)S(1)} %get-tuple-element.24.recv_ref, bf16[64,32,128]{2,1,0:T(8,128)(2,1)S(1)} %bitcast.14, f32[8,128]{1,0:T(8,128)S(1)} %get-tuple-element.26.pot_ref), custom_call_target="tpu_custom_call" | custom-call | tf_op jit(solution)/shard_map/cond/branch_0_fun/store_blocks/pallas_call | solution.py:393
Async XLA Ops:
  0.6 44.1 %copy-start = (s32[48,1]{0,1:T(1,128)S(1)}, s32[48,1]{0,1:T(1,128)}, u32[]{:S(2)}) copy-start(s32[48,1]{0,1:T(1,128)} %param.10) | copy-start | bytes 580
  0.6 44.1 %copy-start.1 = (s32[2,48]{1,0:T(2,128)S(1)}, s32[2,48]{1,0:T(2,128)}, u32[]{:S(2)}) copy-start(s32[2,48]{1,0:T(2,128)} %groups_ref.1) | copy-start | bytes 1156
  0.7 44.1 %copy-start.2 = (s32[48]{0:T(128)S(1)}, s32[48]{0:T(128)}, u32[]{:S(2)}) copy-start(s32[48]{0:T(128)} %param.11) | copy-start | bytes 580
